TPU v7x, 512 devices: a whole 4x8x8 slice. The times are simulated.
512 devices in a mesh: fsdp: 16 (over y_hi, z), roll: 32 (over y_lo, x, core).
Axes of the slice: x: 4, y: 8 (y_hi: 2, y_lo: 4; y = y_hi * 4 + y_lo), z: 8, core: 2. Of those that a mesh axis runs over, the one named last changes fastest.
Arguments:
- hidden: bfloat16 [4, 256, 4096], P(None, 'fsdp', 'roll'), may hold values from -6 to 6
- inner_weight: bfloat16 [4096, 8192], P('fsdp', 'roll'), may hold values from -0.09375 to 0.09375
- gate_weight: bfloat16 [4096, 8192], P('fsdp', 'roll'), may hold values from -0.09375 to 0.09375
- group_weight: bfloat16 [4096, 2048], P('fsdp', 'roll'), may hold values from -0.09375 to 0.09375
- step_weight: bfloat16 [4096, 64], P('fsdp', 'roll'), may hold values from -0.09375 to 0.09375
- output_weight: bfloat16 [8192, 4096], P('roll', 'fsdp'), may hold values from -0.125 to 0.125
- filter_inner: float32 [4, 8192], P(None, 'roll'), may hold values from -3 to 3
- filter_inner_bias: float32 [8192], P('roll'), may hold values from -3 to 3
- filter_group: float32 [4, 2048], P(None, 'roll'), may hold values from -3 to 3
- filter_group_bias: float32 [2048], P('roll'), may hold values from -3 to 3
- step_bias: float32 [64], P('roll'), may hold values from -3 to 0.5
- decay_rate: float32 [64], P('roll'), may hold values from 0.02 to 2
- skip_gain: float32 [64], P('roll'), may hold values from 0.5 to 2
- norm_gain: float32 [8192], P('roll'), may hold values from 0.1 to 1.9
- recurrent_state: bfloat16 [256, 64, 128, 256], P('fsdp', 'roll'), may hold values from -6 to 6
- filter_inner_state: bfloat16 [256, 3, 8192], P('fsdp', None, 'roll'), may hold values from -6 to 6
- filter_group_state: bfloat16 [256, 3, 2048], P('fsdp', None, 'roll'), may hold values from -6 to 6
- live_counts: int32 [16], P('fsdp'), may hold values from 8 to 16, as said below
- target_device: int32 [256], P('fsdp'), may hold values from 0 to 15, as said below
- target_slot: int32 [256], P('fsdp'), may hold values from 0 to 15, as said below
Outputs:
- mixer_output: bfloat16 [4, 256, 4096], P(None, 'fsdp', 'roll')
- new_state: bfloat16 [256, 64, 128, 256], P('fsdp', 'roll')
- new_inner_window: bfloat16 [256, 3, 8192], P('fsdp', None, 'roll')
- new_group_window: bfloat16 [256, 3, 2048], P('fsdp', None, 'roll')
Inputs may be any that keep to these rules, and one draw needn't show every extreme that they name: Each device's live requests are its first live_counts slots; some device has all 16 slots live and another device has exactly the least. `target_device`: no two live source slots share a destination slot; at most 2 live requests of one device go to one device, and some device sends exactly 2 to some device; entries of slots that are not live are of no meaning. `target_slot`: see target_device.
All inputs are finite; a program needn't handle non-finite values.
Results may differ from a plain program's by a relative error of at most 0.034.
Values may be sent and summed in bfloat16 or wider, within the bound.
A program may use at most 64 MiB of HBM per device.

v0:
```python
import jax
import jax.numpy as jnp
from jax import lax
from jax.sharding import PartitionSpec as P

HPG = 16


eps = 1e-05


def causal_filter(prior, fresh, taps, offset_bias):
    sequence = jnp.concatenate(
        [jnp.transpose(prior, (1, 0, 2)).astype(jnp.float32), fresh.astype(jnp.float32)], axis=0
    )
    step_count = fresh.shape[0]
    total = jnp.zeros(fresh.shape, jnp.float32)
    for offset in range(taps.shape[0]):
        total = total + taps[offset] * sequence[offset : offset + step_count]
    filtered = jax.nn.silu(total + offset_bias)
    window = jnp.transpose(sequence[step_count:], (1, 0, 2)).astype(jnp.bfloat16)
    return (filtered, window)


def on_device(
    hidden,
    inner_weight,
    gate_weight,
    group_weight,
    step_weight,
    output_weight,
    filter_inner,
    filter_inner_bias,
    filter_group,
    filter_group_bias,
    step_bias,
    decay_rate,
    skip_gain,
    norm_gain,
    recurrent_state,
    filter_inner_state,
    filter_group_state,
    live_counts,
    target_device,
    target_slot,
):
    width_fsdp = lax.axis_size("fsdp")
    slot_count = recurrent_state.shape[0]
    heads_here = recurrent_state.shape[1]
    head_dim = recurrent_state.shape[2]
    state_dim = recurrent_state.shape[3]
    step_count = hidden.shape[0]
    spread = max(1, min(width_fsdp, slot_count // 2))
    capacity = slot_count // spread
    is_live = jnp.arange(slot_count, dtype=jnp.int32) < live_counts[0]
    matches = is_live[:, None] & (
        target_device[:, None] == jnp.arange(width_fsdp, dtype=jnp.int32)[None, :]
    )
    ranking = jnp.cumsum(matches.astype(jnp.int32), axis=0) - 1
    position = jnp.sum(jnp.where(matches, ranking, 0), axis=1)
    chosen = matches.T[:, None, :] & (
        position[None, None, :] == jnp.arange(capacity, dtype=jnp.int32)[None, :, None]
    )
    picker = chosen.reshape(width_fsdp * capacity, slot_count)
    slot_sent = jnp.sum(jnp.where(picker, target_slot[None, :] + 1, 0), axis=1) - 1
    picker_matrix = picker.astype(jnp.bfloat16)

    def pack_rows(values):
        flat = values.reshape(slot_count, -1)
        packed = jnp.dot(picker_matrix, flat, preferred_element_type=jnp.float32).astype(
            jnp.bfloat16
        )
        return packed.reshape(width_fsdp, capacity, flat.shape[1])

    recv_state, recv_inner, recv_group, recv_slot = (
        lax.all_to_all(pack_rows(recurrent_state), "fsdp", split_axis=0, concat_axis=0, tiled=True),
        lax.all_to_all(
            pack_rows(filter_inner_state), "fsdp", split_axis=0, concat_axis=0, tiled=True
        ),
        lax.all_to_all(
            pack_rows(filter_group_state), "fsdp", split_axis=0, concat_axis=0, tiled=True
        ),
        lax.all_to_all(
            slot_sent.reshape(width_fsdp, capacity), "fsdp", split_axis=0, concat_axis=0, tiled=True
        ),
    )
    placer = (jnp.arange(slot_count, dtype=jnp.int32)[:, None] == recv_slot.reshape(1, -1)).astype(
        jnp.bfloat16
    )

    def place_rows(received, like):
        flat = received.reshape(width_fsdp * capacity, -1)
        return jnp.dot(placer, flat, preferred_element_type=jnp.float32).reshape(like.shape)

    state_now = place_rows(recv_state, recurrent_state)
    prior_inner = place_rows(recv_inner, filter_inner_state).astype(jnp.bfloat16)
    prior_group = place_rows(recv_group, filter_group_state).astype(jnp.bfloat16)
    gathered = lax.all_gather(hidden, "roll", axis=2, tiled=True)
    token_rows = gathered.reshape(step_count * slot_count, gathered.shape[2])
    panel = (
        lax.all_gather(inner_weight, "fsdp", axis=0, tiled=True),
        lax.all_gather(gate_weight, "fsdp", axis=0, tiled=True),
        lax.all_gather(group_weight, "fsdp", axis=0, tiled=True),
        lax.all_gather(step_weight, "fsdp", axis=0, tiled=True),
    )
    pieces = tuple(
        (jnp.dot(token_rows, block, preferred_element_type=jnp.float32) for block in panel)
    )
    inner_raw = pieces[0].astype(jnp.bfloat16).reshape(step_count, slot_count, -1)
    gate_raw = pieces[1].astype(jnp.bfloat16).reshape(step_count, slot_count, -1)
    group_raw = pieces[2].astype(jnp.bfloat16).reshape(step_count, slot_count, -1)
    step_raw = pieces[3].astype(jnp.bfloat16).reshape(step_count, slot_count, -1)
    inner_conv, inner_window = causal_filter(
        prior_inner, inner_raw, filter_inner, filter_inner_bias
    )
    group_conv, group_window = causal_filter(
        prior_group, group_raw, filter_group, filter_group_bias
    )
    group_all = lax.all_gather(group_conv.astype(jnp.bfloat16), "roll", axis=2, tiled=True).astype(
        jnp.float32
    )
    basis_cols = group_all.shape[2] // 2
    group_count = basis_cols // state_dim
    group_index = lax.axis_index("roll") * heads_here // HPG
    input_basis = lax.dynamic_slice_in_dim(group_all, group_index * state_dim, state_dim, 2)
    output_basis = lax.dynamic_slice_in_dim(
        group_all, basis_cols + group_index * state_dim, state_dim, 2
    )
    step_sizes = jax.nn.softplus(step_raw.astype(jnp.float32) + step_bias)
    decays = jnp.exp(-step_sizes * decay_rate)
    inner_values = inner_conv.reshape(step_count, slot_count, heads_here, head_dim)
    carried = state_now
    outputs = []
    for step in range(step_count):
        carried = (
            carried * decays[step][:, :, None, None]
            + (step_sizes[step][:, :, None] * inner_values[step])[..., None]
            * input_basis[step][:, None, None, :]
        )
        readout = jnp.einsum(
            "lhpn,ln->lhp", carried, output_basis[step], precision=lax.Precision.HIGHEST
        )
        outputs.append(readout + skip_gain[None, :, None] * inner_values[step])
    scanned = jnp.stack(outputs).reshape(step_count, slot_count, heads_here * head_dim)
    gated = scanned * jax.nn.silu(gate_raw.astype(jnp.float32))
    local_sum = jnp.sum(gated * gated, axis=2)
    marker = (jnp.arange(group_count, dtype=jnp.int32) == group_index).astype(jnp.float32)
    group_sums = lax.psum(local_sum[:, :, None] * marker, "roll")
    group_total = jnp.sum(group_sums * marker, axis=2)
    scale = lax.rsqrt(group_total / (HPG * head_dim) + eps)
    normed = (
        (gated * scale[:, :, None] * norm_gain)
        .astype(jnp.bfloat16)
        .reshape(step_count * slot_count, -1)
    )
    partial_out = jnp.dot(
        normed,
        lax.all_gather(output_weight, "fsdp", axis=1, tiled=True),
        preferred_element_type=jnp.float32,
    )
    reduced = lax.psum_scatter(
        partial_out.astype(jnp.bfloat16), "roll", scatter_dimension=1, tiled=True
    )
    mixer_output = reduced.reshape(step_count, slot_count, -1)
    return (mixer_output, carried.astype(jnp.bfloat16), inner_window, group_window)


def solution(mesh):
    return jax.shard_map(
        on_device,
        mesh=mesh,
        in_specs=(
            P(None, "fsdp", "roll"),
            P("fsdp", "roll"),
            P("fsdp", "roll"),
            P("fsdp", "roll"),
            P("fsdp", "roll"),
            P("roll", "fsdp"),
            P(None, "roll"),
            P("roll"),
            P(None, "roll"),
            P("roll"),
            P("roll"),
            P("roll"),
            P("roll"),
            P("roll"),
            P("fsdp", "roll", None, None),
            P("fsdp", None, "roll"),
            P("fsdp", None, "roll"),
            P("fsdp"),
            P("fsdp"),
            P("fsdp"),
        ),
        out_specs=(
            P(None, "fsdp", "roll"),
            P("fsdp", "roll", None, None),
            P("fsdp", None, "roll"),
            P("fsdp", None, "roll"),
        ),
        check_vma=False,
    )
```

profile of v0, /device:TPU:64, one launch (start us, length us, event | category | flops | bytes accessed | tf_op | source)
XLA Modules:
  0.0 716.7 jit_solution(9110848239101431427)
XLA Ops:
  7.9 0.7 all-gather.6.cloned.1.call-update
  9.3 0.8 fusion.50
  10.1 0.8 select_reduce_fusion.1
  12.1 0.7 copy.153
  12.8 15.2 %all-to-all-start = ((s32[16,1,2]{2,1,0:T(1,128)}), s32[16,1,2]{2,1,0:T(1,128)S(1)}, u32[]{:S(2)}, u32[]{:S(2)}) async-start(s32[16,1,2]{2,1,0:T(1,128)} %copy.153), calls=%async_computation | async-start | bytes 16384 | tf_op jit(solution)/shard_map/all_to_all | solution.py:83
  28.1 0.7 copy.158
  29.6 0.7 copy.195
  30.4 8.6 %all-to-all-done = s32[16,1,2]{2,1,0:T(1,128)S(1)} async-done(((s32[16,1,2]{2,1,0:T(1,128)}), s32[16,1,2]{2,1,0:T(1,128)S(1)}, u32[]{:S(2)}, u32[]{:S(2)}) %all-to-all-start) | async-done | bytes 160 | tf_op jit(solution)/shard_map/all_to_all | solution.py:83
  39.0 4.7 all-to-all-start.3
  44.5 2.8 copy.196
  47.2 7.7 %all-to-all-done.3 = bf16[16,2,192]{2,1,0:T(2,128)(2,1)S(1)} async-done(((bf16[16,2,192]{2,1,0:T(2,128)(2,1)}), bf16[16,2,192]{2,1,0:T(2,128)(2,1)S(1)}, u32[]{:S(2)}, u32[]{:S(2)}) %all-to-all-start.3) | async-done | bytes 12320 | tf_op jit(solution)/shard_map/all_to_all | solution.py:80
  54.9 4.6 all-to-all-start.2
  59.6 3.2 convolution_convert_fusion
  62.7 6.0 reshape.255
  68.8 2.1 all-to-all-done.2
  70.8 10.2 %all-to-all-start.1 = ((bf16[16,2,65536]{2,1,0:T(2,128)(2,1)}), bf16[16,2,65536]{2,1,0:T(2,128)(2,1)}, u32[]{:S(2)}, u32[]{:S(2)}) async-start(bf16[16,2,65536]{2,1,0:T(2,128)(2,1)} %reshape.255), calls=%async_computation.1 | async-start | bytes 8388608 | tf_op jit(solution)/shard_map/all_to_all | solution.py:76
  81.8 188.5 %all_gather.24 = bf16[4096,64]{0,1:T(8,128)(2,1)S(1)} all-gather(bf16[256,64]{0,1:T(8,128)(2,1)S(1)} %copy-done.10), channel_id=1, replica_groups=mesh['fsdp'=16,'roll'=32] {'fsdp'}, dimensions={0}, use_global_device_ids=true | all-gather | bytes 557056 | tf_op jit(solution)/shard_map/all_gather | solution.py:103
  270.4 42.0 %all_gather.21 = bf16[4,16,4096]{2,1,0:T(8,128)(2,1)S(1)} all-gather(bf16[4,16,128]{2,1,0:T(8,128)(2,1)S(1)} %copy-done.11), channel_id=1, replica_groups=mesh['fsdp'=16,'roll'=32] {'roll'}, dimensions={2}, use_global_device_ids=true | all-gather | bytes 540672 | tf_op jit(solution)/shard_map/all_gather | solution.py:98
  312.6 52.8 %all_gather.22 = bf16[4096,2]{0,1:T(2,128)(2,1)S(1)} all-gather(bf16[256,2]{0,1:T(2,128)(2,1)S(1)} %copy-done.21), channel_id=1, replica_groups=mesh['fsdp'=16,'roll'=32] {'fsdp'}, dimensions={0}, use_global_device_ids=true | all-gather | bytes 17408 | tf_op jit(solution)/shard_map/all_gather | solution.py:104
  368.9 45.4 %all_gather.25 = bf16[4,16,2048]{1,0,2:T(4,128)(2,1)S(1)} all-gather(bf16[4,16,64]{1,0,2:T(4,128)(2,1)S(1)} %copy.160), channel_id=1, replica_groups=mesh['fsdp'=16,'roll'=32] {'roll'}, dimensions={2}, use_global_device_ids=true | all-gather | bytes 270336 | tf_op jit(solution)/shard_map/all_gather | solution.py:119
  417.9 0.7 copy.193
  419.9 0.7 copy.190
  420.8 2.1 convolution_convert_fusion.4
  423.9 0.7 broadcast_multiply_fusion.2
  424.6 1.3 broadcast_multiply_fusion.3
  425.9 5.5 reshape.256
  431.5 3.3 copy.197
  434.9 8.9 %fusion.56 = (bf16[16,2,128,256]{3,0,2,1:T(8,128)(2,1)S(1)}, f32[16,2,128,256]{3,0,2,1:T(8,128)S(1)}, f32[16,2,128,256]{3,0,2,1:T(8,128)}, f32[16,2,128,256]{3,0,2,1:T(8,128)}, f32[16,2,128,256]{3,0,2,1:T(8,128)}) fusion(f32[16,256]{1,0:T(8,128)S(1)} %copy-done.9, f32[16,2,128]{0,2,1:T(8,128)S(1)} %broadcast_multiply_fusion, f32[16,2]{0,1:T(2,128)S(1)} %bitcast.162, ...), kind=kOutput, calls=%fused_computation.114 | convolution fusion | flops 80740864 | bytes 23200384 | tf_op jit(solution)/shard_map/dot_general | solution.py:93
  443.7 4.3 fusion
  448.2 6.3 fusion.2
  454.6 7.2 %fusion.4 = f32[16,1,2,128]{3,1,2,0:T(1,128)} fusion(f32[16,2,128,256]{3,0,2,1:T(8,128)} %get-tuple-element.35, bf16[16,256,1,1]{1,0,2,3:T(8,128)(2,1)S(1)} %bitcast.152), kind=kOutput, calls=%fused_computation.6 | convolution fusion | flops 12582912 | bytes 4218880 | tf_op jit(solution)/shard_map/lhpn,ln->lhp/dot_general | solution.py:140
  461.8 0.8 copy.180
  462.6 6.9 fusion.6
  469.6 1.5 copy.177
  471.0 1.8 bitcast_add_fusion.3
  472.8 1.0 copy.169
  473.8 1.0 copy.170
  474.8 1.0 copy.171
  475.7 1.0 copy.172
  476.8 2.1 multiply_reduce_fusion
  479.0 0.7 broadcast_multiply_fusion.4
  479.7 69.8 %psum.7 = f32[4,16,4]{1,2,0:T(4,128)S(1)} all-reduce(f32[4,16,4]{1,2,0:T(4,128)S(1)} %broadcast_multiply_fusion.4), channel_id=1, replica_groups=mesh['fsdp'=16,'roll'=32] {'roll'}, use_global_device_ids=true, to_apply=%region_4.5 | all-reduce | flops 256 | bytes 2048 | tf_op jit(solution)/shard_map/psum | solution.py:148
  549.5 0.8 multiply_reduce_fusion.1
  550.4 2.1 convolution_convert_fusion.1
  552.5 1.3 copy.187
  555.1 2.0 copy.173
  557.1 151.6 %reduce-scatter.4.cloned.1.call-done = bf16[128,64]{1,0:T(8,128)(2,1)} async-done(((bf16[4096,64]{1,0:T(8,128)(2,1)}), bf16[128,64]{1,0:T(8,128)(2,1)}) %reduce-scatter.4.cloned.1.call-update) | async-done | bytes 16400
  708.7 1.4 copy.188
  (119 shorter events, 15.7 us)
Async XLA Ops:
  7.2 413.6 %all-gather.4.cloned.1.call-start = ((), (), s32[]{:S(2)}) async-start(), calls=%async_computation.5 | async-start | bytes 2228224 | tf_op jit(solution)/shard_map/all_gather | solution.py:101
  7.9 468.8 %all-gather.6.cloned.1.call-start = ((), (), s32[]{:S(2)}) async-start(), calls=%async_computation.6 | async-start | bytes 2228224 | tf_op jit(solution)/shard_map/all_gather | solution.py:102
  12.8 26.2 %all-to-all-start = ((s32[16,1,2]{2,1,0:T(1,128)}), s32[16,1,2]{2,1,0:T(1,128)S(1)}, u32[]{:S(2)}, u32[]{:S(2)}) async-start(s32[16,1,2]{2,1,0:T(1,128)} %copy.153), calls=%async_computation | async-start | bytes 16384 | tf_op jit(solution)/shard_map/all_to_all | solution.py:83
  39.0 16.0 %all-to-all-start.3 = ((bf16[16,2,192]{2,1,0:T(2,128)(2,1)}), bf16[16,2,192]{2,1,0:T(2,128)(2,1)S(1)}, u32[]{:S(2)}, u32[]{:S(2)}) async-start(bf16[16,2,192]{2,1,0:T(2,128)(2,1)} %reshape.262), calls=%async_computation.3 | async-start | bytes 32768 | tf_op jit(solution)/shard_map/all_to_all | solution.py:80
  54.9 15.9 %all-to-all-start.2 = ((bf16[16,2,768]{2,1,0:T(2,128)(2,1)}), bf16[16,2,768]{2,1,0:T(2,128)(2,1)S(1)}, u32[]{:S(2)}, u32[]{:S(2)}) async-start(bf16[16,2,768]{2,1,0:T(2,128)(2,1)} %reshape.259), calls=%async_computation.2 | async-start | bytes 98304 | tf_op jit(solution)/shard_map/all_to_all | solution.py:77
  68.7 13.1 %copy-start.10 = (bf16[256,64]{0,1:T(8,128)(2,1)S(1)}, bf16[256,64]{0,1:T(8,128)(2,1)}, u32[]{:S(2)}) copy-start(bf16[256,64]{0,1:T(8,128)(2,1)} %param.23) | copy-start | bytes 98308
  68.7 201.7 %copy-start.11 = (bf16[4,16,128]{2,1,0:T(8,128)(2,1)S(1)}, bf16[4,16,128]{2,1,0:T(8,128)(2,1)}, u32[]{:S(2)}) copy-start(bf16[4,16,128]{2,1,0:T(8,128)(2,1)} %param.20) | copy-start | bytes 49156
  68.7 243.9 %copy-start.21 = (bf16[256,2]{0,1:T(2,128)(2,1)S(1)}, bf16[256,2]{0,1:T(2,128)(2,1)}, u32[]{:S(2)}) copy-start(bf16[256,2]{0,1:T(2,128)(2,1)} %param.24) | copy-start | bytes 3076
  68.7 297.7 %copy-start.19 = (f32[4,64]{1,0:T(4,128)S(1)}, f32[4,64]{1,0:T(4,128)}, u32[]{:S(2)}) copy-start(f32[4,64]{1,0:T(4,128)} %param.28) | copy-start | bytes 3076
  68.7 297.7 %copy-start.18 = (f32[4,256]{1,0:T(4,128)S(1)}, f32[4,256]{1,0:T(4,128)}, u32[]{:S(2)}) copy-start(f32[4,256]{1,0:T(4,128)} %param.26) | copy-start | bytes 12292
  68.7 297.7 %copy-start.23 = (f32[2]{0:T(128)S(1)}, f32[2]{0:T(128)}, u32[]{:S(2)}) copy-start(f32[2]{0:T(128)} %param.31) | copy-start | bytes 28
  68.8 297.7 %copy-start.24 = (f32[2]{0:T(128)S(1)}, f32[2]{0:T(128)}, u32[]{:S(2)}) copy-start(f32[2]{0:T(128)} %param.30) | copy-start | bytes 28
  68.8 299.9 %copy-start.22 = (f32[64]{0:T(128)S(1)}, f32[64]{0:T(128)}, u32[]{:S(2)}) copy-start(f32[64]{0:T(128)} %param.29) | copy-start | bytes 772
  70.8 355.1 %all-to-all-start.1 = ((bf16[16,2,65536]{2,1,0:T(2,128)(2,1)}), bf16[16,2,65536]{2,1,0:T(2,128)(2,1)}, u32[]{:S(2)}, u32[]{:S(2)}) async-start(bf16[16,2,65536]{2,1,0:T(2,128)(2,1)} %reshape.255), calls=%async_computation.1 | async-start | bytes 8388608 | tf_op jit(solution)/shard_map/all_to_all | solution.py:76
  81.0 469.4 %all-gather.8.cloned.1.call-start = ((), (), s32[]{:S(2)}) async-start(), calls=%async_computation.7 | async-start | bytes 2228224 | tf_op jit(solution)/shard_map/all_gather | solution.py:158
  81.8 626.9 %reduce-scatter.4.cloned.1.call-start = ((), (), s32[]{:S(2)}) async-start(), calls=%async_computation.8 | async-start | bytes 1081344
  368.4 54.4 %copy-start.12 = (s32[32]{0:T(128)}, s32[32]{0:T(128)S(1)}, u32[]{:S(2)}) copy-start(s32[32]{0:T(128)S(1)} %eq.77) | copy-start | bytes 388
  368.8 54.0 %copy-start.20 = (f32[256]{0:T(256)S(1)}, f32[256]{0:T(256)}, u32[]{:S(2)}) copy-start(f32[256]{0:T(256)} %param.27) | copy-start | bytes 3076
  422.8 0.6 copy-start.1
  431.4 3.3 copy-start
  431.4 3.3 copy-start.6
  431.4 3.4 copy-start.7
  431.4 3.4 copy-start.8
  431.4 3.4 copy-start.9
  431.5 3.4 copy-start.13
  431.5 3.4 copy-start.14
  431.5 3.4 copy-start.15
  431.5 3.4 copy-start.16
  431.5 3.4 copy-start.17
  434.9 8.9 %copy-start.5 = (bf16[1,16,256]{2,1,0:T(8,128)(2,1)S(1)}, bf16[1,16,256]{2,1,0:T(8,128)(2,1)}, u32[]{:S(2)}) copy-start(bf16[1,16,256]{2,1,0:T(8,128)(2,1)} %copy.193) | copy-start | bytes 24580
  443.7 4.5 copy-start.4
  443.7 10.9 %copy-start.3 = (bf16[1,16,256]{2,1,0:T(8,128)(2,1)S(1)}, bf16[1,16,256]{2,1,0:T(8,128)(2,1)}, u32[]{:S(2)}) copy-start(bf16[1,16,256]{2,1,0:T(8,128)(2,1)} %copy.191) | copy-start | bytes 24580
  475.7 78.8 %copy-start.2 = (bf16[64,256]{1,0:T(8,128)(2,1)S(1)}, bf16[64,256]{1,0:T(8,128)(2,1)}, u32[]{:S(2)}) copy-start(bf16[64,256]{1,0:T(8,128)(2,1)} %copy-done.1) | copy-start | bytes 98308
Sparse Core Ops, SparseCore 0:
  11.2 188.0 all-gather.3
  202.5 152.5 all-gather.5
  358.1 100.4 all-gather.7
  554.0 154.6 reduce-scatter.3
where the time goes:
time: 718 us; the launch traced here: 717 us
  blocking collectives  399 us (56%)
  waiting for transfers between devices  172 us (24%)
  matrix products  44.1 us (6%)
  local copies, waits for them, and re-layouts  42.5 us (6%)
  starting transfers between devices  34.9 us (5%)
  between operations  14.9 us (2%)
  other arithmetic  9.56 us (1%)
    all_gather x1, blocking collectives, on_device(): lax.all_gather(group_weight, 'fsdp', axis=0, tiled=True)  189 us
    unnamed x5, waiting for transfers between devices  154 us
    psum x1, blocking collectives, on_device(): group_sums = lax.psum(local_sum[:, :, None] * marker, 'roll')  69.8 us
    all_gather x1, blocking collectives, on_device(): lax.all_gather(step_weight, 'fsdp', axis=0, tiled=True)  52.8 us
    all_gather x1, blocking collectives, on_device(): lax.all_gather(group_conv.astype(jnp.bfloat16), 'roll', axis=2, tiled=True)  45.4 us
    all_gather x1, blocking collectives, on_device(): gathered = lax.all_gather(hidden, 'roll', axis=2, tiled=True)  42 us
    dot_general x4, matrix products, on_device(): jnp.einsum('lhpn,ln->lhp', carried, output_basis[step], precision=lax.Pre...  24.8 us
    all_to_all x1, starting transfers between devices, on_device(): lax.all_to_all(slot_sent.reshape(width_fsdp, capacity), 'fsdp', split_axi...  15.2 us
  transfers between devices with their start and end apart: 8, of which 4 were waited for; matrix products, arithmetic and copies ran while one was open for 13% of the time, Pallas kernels for 0%

commit v1 on v0

v1 whole, which is shorter than its diff:
```python
import jax
import jax.numpy as jnp
from jax import lax
from jax.experimental import pallas as pl
from jax.experimental.pallas import tpu as pltpu
from jax.sharding import PartitionSpec as P

MESH = pl.DeviceIdType.MESH
F = 16
R = 32
Z = 8
HPG = 16
NSTEP = 4
SLOTS = 16
EPS = 1e-05
F32 = jnp.float32
BF16 = jnp.bfloat16


def peer_of(f, o):
    return ((f // Z + o // Z) % 2) * Z + (f % Z + o % Z) % Z


def source_of(f, o):
    return ((f // Z + o // Z) % 2) * Z + (f % Z + Z - o % Z) % Z


def silu(v):
    return v / (1.0 + jnp.exp(-v))


def dot(a, b, dims):
    return lax.dot_general(a, b, (dims, ((), ())), preferred_element_type=F32)


def kernel(
    idx, hid, wi, wg, wgs, wo, par, winp, state,
    out, new_state, win_i, win_g,
    hid_all, p_send, p_recv, w_recv, w32, st_v, st_send, st_recv, gc_send, gc_recv,
    ga_all, po_send, po_recv, fin_send, fin_recv, acc, ck, bk, uk, yk, ssum, jq,
    h1_s, h1_r, h2_s, h2_r, w_s, w_r, st_s, st_r, p_s, p_r, gc_s, gc_r, ga_s, ga_r, po_s, po_r, fin_s, fin_r, loc,
):
    f = lax.axis_index("fsdp")
    r = lax.axis_index("roll")
    half = r % 2
    home = r // 2

    def remote(src, dst, s, d, device):
        return pltpu.make_async_remote_copy(
            src_ref=src, dst_ref=dst, send_sem=s, recv_sem=d, device_id=device, device_id_type=MESH
        )

    load_state = pltpu.make_async_copy(state, st_v, loc.at[0])
    load_state.start()

    barrier = pltpu.get_barrier_semaphore()

    @pl.loop(1, F)
    def _(o):
        pl.semaphore_signal(barrier, inc=1, device_id=(peer_of(f, o), r), device_id_type=MESH)

    @pl.loop(1, R)
    def _(o):
        pl.semaphore_signal(barrier, inc=1, device_id=(f, (r + o) % R), device_id_type=MESH)

    def is_self(k):
        return (home == f) & (half == k)

    @pl.when(home != f)
    def _():
        for k in range(2):
            pl.semaphore_signal(barrier, inc=1, device_id=(home, 2 * f + k), device_id_type=MESH)

    pl.semaphore_wait(barrier, F - 1 + R - 1 + jnp.where(home != f, 2, 0))

    for k in range(2):

        @pl.when(jnp.logical_not(is_self(k)))
        def _():
            remote(
                hid.at[pl.ds(32 * k, 32)], hid_all.at[2 * f + k, half], h1_s.at[k], h1_r.at[half],
                (home, 2 * f + k),
            ).start()

        @pl.when(is_self(k))
        def _():
            hid_all[r, k] = hid[pl.ds(32 * k, 32), :]

    for k in range(2):

        @pl.when(jnp.logical_not(is_self(k)))
        def _():
            remote(hid.at[pl.ds(0, 32)], hid_all.at[r, k], h1_s.at[k], h1_r.at[k], (f, r)).wait_recv()

    @pl.loop(1, R)
    def _(o):
        to = (r + o) % R
        remote(hid_all.at[r], hid_all.at[r], h2_s.at[to], h2_r.at[r], (f, to)).start()

    @pl.loop(1, F)
    def _(o):
        d = peer_of(f, o)
        remote(winp.at[d], w_recv.at[f], w_s.at[d], w_r.at[f], (d, r)).start()

    w_recv[f] = winp[f]
    load_state.wait()

    @pl.loop(1, F)
    def _(o):
        d = peer_of(f, o)
        for c in range(2):
            st_send[2 * d + c] = st_v[idx[2 * d + c]]
        remote(
            st_send.at[pl.ds(2 * d, 2)], st_recv.at[pl.ds(2 * f, 2)], st_s.at[d], st_r.at[f], (d, r)
        ).start()

    for c in range(2):
        st_recv[2 * f + c] = st_v[idx[2 * f + c]]

    def project(d):
        for h in range(2):
            chunk = 2 * d + h

            @pl.when(chunk != r)
            def _():
                remote(
                    hid_all.at[chunk], hid_all.at[chunk], h2_s.at[chunk], h2_r.at[chunk], (f, r)
                ).wait_recv()

        rows = jnp.concatenate(
            [
                jnp.concatenate([hid_all[2 * d + h, 0], hid_all[2 * d + h, 1]], axis=1)
                for h in range(2)
            ],
            axis=0,
        )
        nn = ((1,), (0,))
        return (
            dot(rows, wi[...], nn).astype(BF16),
            dot(rows, wg[...], nn).astype(BF16),
            dot(rows, wgs[...], nn).astype(BF16),
        )

    @pl.loop(1, F)
    def _(o):
        d = peer_of(f, o)
        a, b, c = project(d)
        p_send[d, :, 0:256] = a
        p_send[d, :, 256:512] = b
        p_send[d, :, 512:640] = c
        remote(p_send.at[d], p_recv.at[f], p_s.at[d], p_r.at[f], (d, r)).start()

    a, b, c = project(f)
    acc[:, 0:256] = a.astype(F32)
    acc[:, 256:512] = b.astype(F32)
    acc[:, 512:640] = c.astype(F32)

    @pl.loop(1, F)
    def _(o):
        s = source_of(f, o)
        remote(winp.at[s], w_recv.at[s], w_s.at[s], w_r.at[s], (f, r)).wait_recv()

    w32[...] = w_recv[...].astype(F32)
    lane = lax.broadcasted_iota(jnp.int32, (F, 128), 1)
    row = lax.broadcasted_iota(jnp.int32, (F, 128), 0)
    placers = []
    code = jnp.zeros((F, 128), F32)
    for c in range(2):
        slot = w32[:, 8 * c + 7, :][:, 64:65].astype(jnp.int32)
        hit = slot == lane
        placers.append(hit.astype(F32).astype(BF16))
        code = code + jnp.where(hit, (2 * row + c + 1).astype(F32), 0.0)

    @pl.loop(0, SLOTS)
    def _(q):
        jq[q] = jnp.sum(jnp.where(lane == q, code, 0.0)).astype(jnp.int32) - 1

    moved = []
    for block in range(8):
        total = jnp.zeros((128, 128), F32)
        for c in range(2):
            total = total + dot(placers[c], w32[:, 8 * c + block, :].astype(BF16), ((0,), (0,)))
        moved.append(total[0:SLOTS])
    prior_i = [jnp.concatenate([moved[2 * k], moved[2 * k + 1]], axis=1) for k in range(3)]
    prior_g = [moved[6], pltpu.roll(moved[6], 64, 1), moved[7]]

    @pl.loop(1, F)
    def _(o):
        s = source_of(f, o)
        remote(p_send.at[s], p_recv.at[s], p_s.at[s], p_r.at[s], (f, r)).wait_recv()
        acc[...] += p_recv[s].astype(F32)

    raw = acc[...].astype(BF16)
    win_i[...] = raw[SLOTS:, 0:256]
    win_g[...] = raw[SLOTS:, 512:640]
    raw = raw.astype(F32)

    def conv(prior, fresh, taps, bias):
        steps = prior + [fresh[SLOTS * t : SLOTS * (t + 1)] for t in range(NSTEP)]
        got = []
        for t in range(NSTEP):
            total = bias
            for k in range(4):
                total = total + taps[k] * steps[t + k]
            got.append(silu(total))
        return got

    group = jnp.concatenate(
        conv(prior_g, raw[:, 512:640], [par[9 + k : 10 + k, 0:128] for k in range(4)], par[13:14, 0:128]),
        axis=0,
    )
    gc_send[...] = jnp.where(half == 1, pltpu.roll(group, 64, 1), group).astype(BF16)
    piece = (r // 16) * 4 + r % 4
    first_user = 8 * ((r % 16) // 4)

    @pl.loop(0, 8)
    def _(m):
        to = first_user + m

        @pl.when(to != r)
        def _():
            remote(gc_send, gc_recv.at[piece], gc_s.at[m], gc_r.at[piece], (f, to)).start()

        @pl.when(to == r)
        def _():
            gc_recv[piece] = gc_send[...]

    xs = conv(prior_i, raw[:, 0:256], [par[k : k + 1] for k in range(4)], par[4:5])
    step_raw = jnp.concatenate(
        [
            jnp.broadcast_to(raw[:, 576:577], (NSTEP * SLOTS, 128)),
            jnp.broadcast_to(raw[:, 577:578], (NSTEP * SLOTS, 128)),
        ],
        axis=1,
    )
    v = step_raw + par[7:8]
    dt = jnp.maximum(v, 0.0) + jnp.log1p(jnp.exp(-jnp.abs(v)))
    dec = jnp.exp(-dt * par[8:9])
    dts = [dt[SLOTS * t : SLOTS * (t + 1)] for t in range(NSTEP)]
    decs = [dec[SLOTS * t : SLOTS * (t + 1)] for t in range(NSTEP)]

    @pl.loop(0, 8)
    def _(i):
        s = (i // 4) * 16 + 4 * (r // 8) + i % 4

        @pl.when(s != r)
        def _():
            remote(gc_send, gc_recv.at[i], gc_s.at[i], gc_r.at[i], (f, r)).wait_recv()

    def basis(i):
        return jnp.concatenate(
            [
                gc_recv[i].astype(F32) + gc_recv[i + 1].astype(F32),
                gc_recv[i + 2].astype(F32) + gc_recv[i + 3].astype(F32),
            ],
            axis=1,
        )

    b_all, c_all = basis(0), basis(4)
    bs = [b_all[SLOTS * t : SLOTS * (t + 1)] for t in range(NSTEP)]
    cs = [c_all[SLOTS * t : SLOTS * (t + 1)] for t in range(NSTEP)]
    us = [dts[t] * xs[t] for t in range(NSTEP)]
    ck[...] = jnp.zeros(ck.shape, F32)
    bk[...] = jnp.zeros(bk.shape, F32)
    uk[...] = jnp.zeros(uk.shape, F32)
    for t in range(NSTEP):
        ck[:, t, :] = cs[t]
        bk[:, t, :] = bs[t]
    tail = None
    for t in reversed(range(NSTEP)):
        uk[:, t, :] = us[t] if tail is None else us[t] * tail
        tail = decs[t] if tail is None else decs[t] * tail
    uk[:, 4, :] = tail

    @pl.loop(1, F)
    def _(o):
        s = source_of(f, o)
        rows = pl.ds(2 * s, 2)
        remote(st_send.at[rows], st_recv.at[rows], st_s.at[s], st_r.at[s], (f, r)).wait_recv()

    @pl.loop(0, SLOTS)
    def _(q):
        j = jq[q]
        start = st_recv[jnp.clip(j, 0, 2 * F - 1)]
        y = dot(ck[q].astype(BF16), start, ((1,), (1,)))
        yk[q] = jnp.where(j >= 0, y, 0.0)

    gates = silu(raw[:, 256:512])
    gated = []
    for t in range(NSTEP):
        total = None
        grown = None
        for s in reversed(range(t + 1)):
            pair = jnp.sum(bs[s] * cs[t], axis=1, keepdims=True)
            term = us[s] * pair
            if grown is not None:
                term = term * grown
            total = term if total is None else total + term
            grown = decs[s] if grown is None else grown * decs[s]
        total = total + grown * yk[:, t, :] + par[6:7] * xs[t]
        gated.append(total * gates[SLOTS * t : SLOTS * (t + 1)])
    ga_all[f] = jnp.concatenate(gated, axis=0).astype(BF16)

    @pl.loop(1, F)
    def _(o):
        d = peer_of(f, o)
        remote(ga_all.at[f], ga_all.at[f], ga_s.at[d], ga_r.at[f], (d, r)).start()

    @pl.loop(0, SLOTS)
    def _(q):
        j = jq[q]
        start = st_recv[jnp.clip(j, 0, 2 * F - 1)].astype(F32)
        start = jnp.where(j >= 0, start, 0.0)
        u = uk[q]
        rate = u[4:5]
        keep = lax.broadcasted_iota(jnp.int32, (8, 256), 0) < 4
        u = jnp.where(keep, u, 0.0)
        high = u.astype(BF16)
        low = (u - high.astype(F32)).astype(BF16)
        b = bk[q].astype(BF16)
        added = dot(
            jnp.concatenate([high, low], axis=0), jnp.concatenate([b, b], axis=0), ((0,), (0,))
        )
        for h in range(2):
            rows = slice(128 * h, 128 * h + 128)
            factor = jnp.concatenate([rate[:, rows], rate[:, rows]], axis=1)
            new_state[q, rows, :] = (start[rows] * factor + added[rows]).astype(BF16)

    def project_out(d):
        g = ga_all[d].astype(F32)
        squares = jnp.sum(g * g, axis=1, keepdims=True)
        part = dot((g * par[5:6]).astype(BF16), wo[...], ((1,), (0,))).astype(BF16)
        where = lax.broadcasted_iota(jnp.int32, (16, 128), 1)
        high = squares.astype(BF16).astype(F32)
        low = squares - high
        for h in range(2):
            at = 32 * h
            lines = [
                jnp.where(where % 64 < 32, high[at + 16 * e : at + 16 * e + 16], low[at + 16 * e : at + 16 * e + 16])
                for e in range(2)
            ]
            squares_tile = jnp.where(where < 64, lines[0], lines[1]).astype(BF16)
            chunk = 2 * d + h
            po_send[chunk, 0:32, :] = part[at : at + 32, 0:128]
            po_send[chunk, 32:64, :] = part[at : at + 32, 128:256]
            po_send[chunk, 64:80, :] = squares_tile

            @pl.when(chunk != r)
            def _():
                remote(po_send.at[chunk], po_recv.at[r], po_s.at[chunk], po_r.at[r], (f, chunk)).start()

            @pl.when(chunk == r)
            def _():
                po_recv[r] = po_send[r]

    project_out(f)

    @pl.loop(1, F)
    def _(o):
        s = source_of(f, o)
        remote(ga_all.at[s], ga_all.at[s], ga_s.at[s], ga_r.at[s], (f, r)).wait_recv()
        project_out(s)

    acc[0:32, 0:256] = jnp.zeros((32, 256), F32)

    @pl.loop(0, 4)
    def _(g):
        acc[32:64, 0:256] = jnp.zeros((32, 256), F32)
        ssum[...] = jnp.zeros((16, 128), F32)

        @pl.loop(0, 8)
        def _(i):
            s = 8 * g + i

            @pl.when(s != r)
            def _():
                remote(po_send.at[s], po_recv.at[s], po_s.at[s], po_r.at[s], (f, r)).wait_recv()

            acc[32:64, 0:128] += po_recv[s, 0:32, :].astype(F32)
            acc[32:64, 128:256] += po_recv[s, 32:64, :].astype(F32)
            ssum[...] += po_recv[s, 64:80, :].astype(F32)

        squares = ssum[...]
        squares = jnp.concatenate(
            [squares[:, 0:1] + squares[:, 32:33], squares[:, 64:65] + squares[:, 96:97]], axis=0
        )
        scale = lax.rsqrt(squares / (HPG * 128) + EPS)
        acc[0:32, 0:256] += acc[32:64, 0:256] * scale

    for k in range(2):
        fin_send[k] = acc[0:32, 128 * k : 128 * k + 128].astype(BF16)

        @pl.when(jnp.logical_not(is_self(k)))
        def _():
            remote(
                fin_send.at[k], fin_recv.at[half], fin_s.at[k], fin_r.at[half], (home, 2 * f + k)
            ).start()

        @pl.when(is_self(k))
        def _():
            fin_recv[k] = fin_send[k]

    for k in range(2):

        @pl.when(jnp.logical_not(is_self(k)))
        def _():
            remote(fin_send.at[k], fin_recv.at[k], fin_s.at[k], fin_r.at[k], (f, r)).wait_recv()

        out[32 * k : 32 * k + 32, :] = fin_recv[k]

    for k in range(2):

        @pl.when(jnp.logical_not(is_self(k)))
        def _():
            remote(hid.at[pl.ds(0, 32)], hid_all.at[r, k], h1_s.at[k], h1_r.at[k], (f, r)).wait_send()
            remote(fin_send.at[k], fin_recv.at[k], fin_s.at[k], fin_r.at[k], (f, r)).wait_send()

    @pl.loop(1, R)
    def _(o):
        to = (r + o) % R
        remote(hid_all.at[r], hid_all.at[r], h2_s.at[to], h2_r.at[r], (f, r)).wait_send()
        remote(po_send.at[to], po_recv.at[r], po_s.at[to], po_r.at[r], (f, r)).wait_send()

    @pl.loop(1, F)
    def _(o):
        d = peer_of(f, o)
        remote(winp.at[d], w_recv.at[f], w_s.at[d], w_r.at[f], (f, r)).wait_send()
        rows = pl.ds(2 * d, 2)
        remote(st_send.at[rows], st_recv.at[rows], st_s.at[d], st_r.at[f], (f, r)).wait_send()
        remote(p_send.at[d], p_recv.at[f], p_s.at[d], p_r.at[f], (f, r)).wait_send()
        remote(ga_all.at[f], ga_all.at[f], ga_s.at[d], ga_r.at[f], (f, r)).wait_send()

    @pl.loop(0, 8)
    def _(m):
        @pl.when(first_user + m != r)
        def _():
            remote(gc_send, gc_recv.at[piece], gc_s.at[m], gc_r.at[piece], (f, r)).wait_send()


def mixer(idx, hid, wi, wg, wgs, wo, par, winp, state):
    vmem = pl.BlockSpec(memory_space=pltpu.VMEM)
    dma = pltpu.SemaphoreType.DMA
    pairs = [2, R, F, F, F, 8, F, R, 2]
    return pl.pallas_call(
        kernel,
        out_shape=(
            jax.ShapeDtypeStruct((64, 128), BF16),
            jax.ShapeDtypeStruct((SLOTS, 256, 256), BF16),
            jax.ShapeDtypeStruct((48, 256), BF16),
            jax.ShapeDtypeStruct((48, 128), BF16),
        ),
        in_specs=[pl.BlockSpec(memory_space=pltpu.SMEM)] + [vmem] * 7 + [pl.BlockSpec(memory_space=pl.ANY)],
        out_specs=(vmem,) * 4,
        scratch_shapes=[
            pltpu.VMEM((R, 2, 32, 128), BF16),
            pltpu.VMEM((F, 64, 640), BF16),
            pltpu.VMEM((F, 64, 640), BF16),
            pltpu.VMEM((F, 16, 128), BF16),
            pltpu.VMEM((F, 16, 128), F32),
            pltpu.VMEM((SLOTS, 256, 256), BF16),
            pltpu.VMEM((2 * F, 256, 256), BF16),
            pltpu.VMEM((2 * F, 256, 256), BF16),
            pltpu.VMEM((64, 128), BF16),
            pltpu.VMEM((8, 64, 128), BF16),
            pltpu.VMEM((F, 64, 256), BF16),
            pltpu.VMEM((R, 80, 128), BF16),
            pltpu.VMEM((R, 80, 128), BF16),
            pltpu.VMEM((2, 32, 128), BF16),
            pltpu.VMEM((2, 32, 128), BF16),
            pltpu.VMEM((64, 640), F32),
            pltpu.VMEM((SLOTS, 8, 256), F32),
            pltpu.VMEM((SLOTS, 8, 256), F32),
            pltpu.VMEM((SLOTS, 8, 256), F32),
            pltpu.VMEM((SLOTS, 8, 256), F32),
            pltpu.VMEM((16, 128), F32),
            pltpu.SMEM((SLOTS,), jnp.int32),
        ]
        + [dma((n,)) for n in pairs for _ in range(2)]
        + [dma((1,))],
        compiler_params=pltpu.CompilerParams(
            collective_id=0, has_side_effects=True, vmem_limit_bytes=48 * 2**20
        ),
        name="mixer",
    )(idx, hid, wi, wg, wgs, wo, par, winp, state)


def on_device(
    hidden,
    inner_weight,
    gate_weight,
    group_weight,
    step_weight,
    output_weight,
    filter_inner,
    filter_inner_bias,
    filter_group,
    filter_group_bias,
    step_bias,
    decay_rate,
    skip_gain,
    norm_gain,
    recurrent_state,
    filter_inner_state,
    filter_group_state,
    live_counts,
    target_device,
    target_slot,
):
    slot = jnp.arange(SLOTS, dtype=jnp.int32)
    device = jnp.arange(F, dtype=jnp.int32)
    match = (slot < live_counts[0])[:, None] & (target_device[:, None] == device[None, :])
    earlier = jnp.sum(
        (match[:, None, :] & (slot[:, None] < slot[None, :])[:, :, None]).astype(jnp.int32), axis=0
    )
    chosen = match[:, :, None] & (earlier[:, :, None] == jnp.arange(2, dtype=jnp.int32))
    picker = chosen.reshape(SLOTS, 2 * F)
    idx = jnp.sum(jnp.where(picker, slot[:, None], 0), axis=0)
    sent_slot = jnp.sum(jnp.where(picker, target_slot[:, None] + 1, 0), axis=0) - 1
    flat = jnp.concatenate(
        [filter_inner_state.reshape(SLOTS, 768), filter_group_state.reshape(SLOTS, 192)], axis=1
    )
    packed = lax.dot_general(
        picker.astype(BF16), flat, (((0,), (0,)), ((), ())), preferred_element_type=F32
    ).astype(BF16)
    slot_columns = jnp.broadcast_to(sent_slot[:, None], (2 * F, 64)).astype(BF16)
    winp = jnp.concatenate([packed, slot_columns], axis=1).reshape(F, 16, 128)

    def head_row(values):
        return jnp.repeat(values, 128).reshape(1, 256)

    par = jnp.concatenate(
        [
            filter_inner,
            filter_inner_bias.reshape(1, 256),
            norm_gain.reshape(1, 256),
            head_row(skip_gain),
            head_row(step_bias),
            head_row(decay_rate),
            jnp.pad(filter_group, ((0, 0), (0, 192))),
            jnp.pad(filter_group_bias.reshape(1, 64), ((0, 0), (0, 192))),
            jnp.zeros((2, 256), F32),
        ],
        axis=0,
    )
    wgs = jnp.concatenate([group_weight, step_weight, jnp.zeros((256, 62), BF16)], axis=1)
    out, new_state, win_i, win_g = mixer(
        idx,
        hidden.reshape(64, 128),
        inner_weight,
        gate_weight,
        wgs,
        output_weight,
        par,
        winp,
        recurrent_state.reshape(SLOTS, 256, 256),
    )
    return (
        out.reshape(NSTEP, SLOTS, 128),
        new_state.reshape(SLOTS, 2, 128, 256),
        jnp.transpose(win_i.reshape(3, SLOTS, 256), (1, 0, 2)),
        jnp.transpose(win_g[:, 0:64].reshape(3, SLOTS, 64), (1, 0, 2)),
    )


def solution(mesh):
    return jax.shard_map(
        on_device,
        mesh=mesh,
        in_specs=(
            P(None, "fsdp", "roll"),
            P("fsdp", "roll"),
            P("fsdp", "roll"),
            P("fsdp", "roll"),
            P("fsdp", "roll"),
            P("roll", "fsdp"),
            P(None, "roll"),
            P("roll"),
            P(None, "roll"),
            P("roll"),
            P("roll"),
            P("roll"),
            P("roll"),
            P("roll"),
            P("fsdp", "roll", None, None),
            P("fsdp", None, "roll"),
            P("fsdp", None, "roll"),
            P("fsdp"),
            P("fsdp"),
            P("fsdp"),
        ),
        out_specs=(
            P(None, "fsdp", "roll"),
            P("fsdp", "roll", None, None),
            P("fsdp", None, "roll"),
            P("fsdp", None, "roll"),
        ),
        check_vma=False,
    )
```

time: 718 us -> 321 us (0.45)
  the two profiles are of different devices: /device:TPU:64 before, /device:TPU:63 now
where the time goes in v1:
time: 321 us
  Pallas kernels  300 us (93%)
  local copies, waits for them, and re-layouts  16.3 us (5%)
    pallas_call x1, Pallas kernels, mixer(): pl.pallas_call(kernel, out_shape=(jax.ShapeDtypeStruct((64, 128), BF16),...  300 us
    unnamed x17, local copies, waits for them, and re-layouts  10.6 us

profile of v1, /device:TPU:63, one launch (start us, length us, event | category | flops | bytes accessed | tf_op | source)
XLA Modules:
  0.0 320.5 jit_solution(17382684401393470682)
XLA Ops:
  1.3 0.7 broadcast_add_fusion
  2.0 0.1 pad.16.clone
  2.0 0.7 pad.9
  2.7 0.7 broadcast_in_dim.55
  3.4 0.7 broadcast_in_dim.56
  4.1 0.7 broadcast_in_dim.54
  4.9 0.7 fusion.6
  5.5 0.1 copy.31
  5.6 0.1 convert_reduce_fusion
  5.7 0.1 copy.32
  5.8 0.7 pad.8
  6.5 0.8 concatenate.13.par
  7.3 0.1 eq.58
  7.4 0.6 select_reduce_fusion
  8.0 0.1 convert_element_type.21
  8.1 0.1 reduce_sum.31.idx
  8.2 0.1 broadcast_in_dim.59
  8.3 0.7 copy.36
  9.0 0.1 reshape.164
  9.1 0.7 copy.37
  9.8 0.2 convolution_convert_fusion
  10.0 0.1 pad_maximum_fusion
  10.2 0.9 copy.33
  11.1 0.8 copy.34
  11.9 0.1 maximum_maximum_fusion.wgs
  12.0 0.0 copy-start
  12.0 1.6 copy-done
  13.6 0.0 copy-start.1
  13.6 0.9 copy-done.1
  14.5 0.0 copy-start.2
  14.5 0.9 copy-done.2
  15.4 0.0 copy-start.3
  15.4 0.9 copy-done.3
  16.3 0.0 copy-start.4
  16.3 0.7 copy-done.4
  17.0 300.4 %mixer.1 = (bf16[64,128]{1,0:T(8,128)(2,1)S(1)}, bf16[16,256,256]{2,1,0:T(8,128)(2,1)S(1)}, bf16[48,256]{1,0:T(8,128)(2,1)S(1)}, bf16[48,128]{1,0:T(8,128)(2,1)S(1)}) custom-call(s32[32]{0:T(128)S(1)} %reduce_sum.31.idx, bf16[64,128]{1,0:T(8,128)(2,1)S(1)} %bitcast.27, bf16[256,256]{1,0:T(8,128)(2,1)S(1)} %copy-done.1, bf16[256,256]{1,0:T(8,128)(2,1)S(1)} %copy-done.2, ...), custom_call_target="tpu_custom_call" | custom-call | tf_op jit(solution)/shard_map/mixer/pallas_call | solution.py:444
  317.4 0.6 copy.44
  318.0 1.3 copy.45
  319.3 0.6 copy.46
  319.9 0.6 copy.47
  (10 shorter events, 0.1 us)
Async XLA Ops:
  12.0 1.6 copy-start
  13.6 0.9 copy-start.1
  14.5 0.9 copy-start.2
  15.4 0.9 copy-start.3
  16.3 0.7 copy-start.4

commit v2 on v1

--- a/solution.py
+++ b/solution.py
@@ -13,6 +13,7 @@
 NSTEP = 4
 SLOTS = 16
 EPS = 1e-05
+EARLY = 4
 F32 = jnp.float32
 BF16 = jnp.bfloat16
 
@@ -25,6 +26,12 @@
     return ((f // Z + o // Z) % 2) * Z + (f % Z + Z - o % Z) % Z
 
 
+def order(i):
+    g, m = i // 4 + 1, i % 4
+    near = (m // 2) * Z + jnp.where(m % 2 == 0, g, Z - g)
+    return jnp.where(i < 12, near, jnp.where(i == 12, Z, 4 + Z * (i - 13)))
+
+
 def silu(v):
     return v / (1.0 + jnp.exp(-v))
 
@@ -34,8 +41,11 @@
 
 
 def kernel(
-    idx, hid, wi, wg, wgs, wo, par, winp, state,
+    live_h, td_h, ts_h, sb_h, dr_h, sg_h, hid_h, wi_h, wg_h, wgr_h, wst_h, wo_h, fi_h, fib_h, fg_h, fgb_h, gain_h,
+    wini_h, wing_h, state,
     out, new_state, win_i, win_g,
+    live, td, ts, sb, dr, sg, hid, wi, wg, wgr, wst, wo, fi, fib, fg, fgb, gain, wini, wing,
+    wgs, gpar, win32, w_send, wg32,
     hid_all, p_send, p_recv, w_recv, w32, st_v, st_send, st_recv, gc_send, gc_recv,
     ga_all, po_send, po_recv, fin_send, fin_recv, acc, ck, bk, uk, yk, ssum, jq,
     h1_s, h1_r, h2_s, h2_r, w_s, w_r, st_s, st_r, p_s, p_r, gc_s, gc_r, ga_s, ga_r, po_s, po_r, fin_s, fin_r, loc,
@@ -50,8 +60,14 @@
             src_ref=src, dst_ref=dst, send_sem=s, recv_sem=d, device_id=device, device_id_type=MESH
         )
 
-    load_state = pltpu.make_async_copy(state, st_v, loc.at[0])
-    load_state.start()
+    pairs = [
+        (hid_h, hid), (td_h, td), (ts_h, ts), (live_h, live), (state, st_v), (wini_h, wini), (wing_h, wing),
+        (wi_h, wi), (wg_h, wg), (wgr_h, wgr), (wst_h, wst), (fi_h, fi), (fib_h, fib), (fg_h, fg), (fgb_h, fgb),
+        (sb_h, sb), (dr_h, dr), (sg_h, sg), (wo_h, wo), (gain_h, gain),
+    ]
+    loads = [pltpu.make_async_copy(a, b, loc.at[i]) for i, (a, b) in enumerate(pairs)]
+    for load in loads:
+        load.start()
 
     barrier = pltpu.get_barrier_semaphore()
 
@@ -71,6 +87,51 @@
         for k in range(2):
             pl.semaphore_signal(barrier, inc=1, device_id=(home, 2 * f + k), device_id_type=MESH)
 
+    for load in loads[1:4] + loads[5:15]:
+        load.wait()
+    wgs[...] = jnp.zeros((128, 256), BF16)
+    wgs[0:64, :] = wgr[...]
+    wgs[64:66, :] = wst[...]
+    gpar[...] = jnp.zeros((8, 128), F32)
+    gpar[0:4, 0:64] = fg[...]
+    gpar[4:5, 0:64] = fgb[...]
+    for k in range(3):
+        win32[:, 2 * k, :] = wini[k, :, 0:128].astype(F32)
+        win32[:, 2 * k + 1, :] = wini[k, :, 128:256].astype(F32)
+    wg32[...] = jnp.zeros((3, SLOTS, 128), F32)
+    for k in range(3):
+        wg32[k, :, 0:64] = wing[k].astype(F32)
+    win32[:, 6, :] = wg32[0] + pltpu.roll(wg32[1], 64, 1)
+    win32[:, 7, :] = wg32[2]
+
+    def picks(d):
+        count = jnp.int32(0)
+        got = [jnp.int32(0), jnp.int32(0)]
+        to = [jnp.int32(-1), jnp.int32(-1)]
+        for i in range(SLOTS):
+            hit = (i < live[0]) & (td[i] == d)
+            for c in range(2):
+                mine = hit & (count == c)
+                got[c] = jnp.where(mine, i, got[c])
+                to[c] = jnp.where(mine, ts[i], to[c])
+            count = count + jnp.where(hit, 1, 0)
+        return got, to
+
+    row8 = lax.broadcasted_iota(jnp.int32, (8, 128), 0)
+    lane8 = lax.broadcasted_iota(jnp.int32, (8, 128), 1)
+
+    @pl.loop(0, F)
+    def _(d):
+        got, to = picks(d)
+        w_send[d] = jnp.concatenate(
+            [
+                jnp.where((row8 == 7) & (lane8 >= 64), to[c].astype(F32), win32[got[c]])
+                for c in range(2)
+            ],
+            axis=0,
+        ).astype(BF16)
+
+    loads[0].wait()
     pl.semaphore_wait(barrier, F - 1 + R - 1 + jnp.where(home != f, 2, 0))
 
     for k in range(2):
@@ -86,6 +147,28 @@
         def _():
             hid_all[r, k] = hid[pl.ds(32 * k, 32), :]
 
+    @pl.loop(0, F - 1)
+    def _(i):
+        d = peer_of(f, order(i))
+        remote(w_send.at[d], w_recv.at[f], w_s.at[d], w_r.at[f], (d, r)).start()
+
+    w_recv[f] = w_send[f]
+
+    loads[4].wait()
+
+    def send_states(i):
+        d = peer_of(f, order(i))
+        got, _ = picks(d)
+        for c in range(2):
+            st_send[2 * d + c] = st_v[got[c]]
+        remote(
+            st_send.at[pl.ds(2 * d, 2)], st_recv.at[pl.ds(2 * f, 2)], st_s.at[d], st_r.at[f], (d, r)
+        ).start()
+
+    @pl.loop(0, EARLY)
+    def _(i):
+        send_states(i)
+
     for k in range(2):
 
         @pl.when(jnp.logical_not(is_self(k)))
@@ -97,25 +180,13 @@
         to = (r + o) % R
         remote(hid_all.at[r], hid_all.at[r], h2_s.at[to], h2_r.at[r], (f, to)).start()
 
-    @pl.loop(1, F)
-    def _(o):
-        d = peer_of(f, o)
-        remote(winp.at[d], w_recv.at[f], w_s.at[d], w_r.at[f], (d, r)).start()
-
-    w_recv[f] = winp[f]
-    load_state.wait()
-
-    @pl.loop(1, F)
-    def _(o):
-        d = peer_of(f, o)
-        for c in range(2):
-            st_send[2 * d + c] = st_v[idx[2 * d + c]]
-        remote(
-            st_send.at[pl.ds(2 * d, 2)], st_recv.at[pl.ds(2 * f, 2)], st_s.at[d], st_r.at[f], (d, r)
-        ).start()
-
+    @pl.loop(EARLY, F - 1)
+    def _(i):
+        send_states(i)
+
+    got, _ = picks(f)
     for c in range(2):
-        st_recv[2 * f + c] = st_v[idx[2 * f + c]]
+        st_recv[2 * f + c] = st_v[got[c]]
 
     def project(d):
         for h in range(2):
@@ -138,12 +209,12 @@
         return (
             dot(rows, wi[...], nn).astype(BF16),
             dot(rows, wg[...], nn).astype(BF16),
-            dot(rows, wgs[...], nn).astype(BF16),
+            dot(rows, wgs[...], ((1,), (1,))).astype(BF16),
         )
 
-    @pl.loop(1, F)
-    def _(o):
-        d = peer_of(f, o)
+    @pl.loop(0, F - 1)
+    def _(i):
+        d = peer_of(f, order(i))
         a, b, c = project(d)
         p_send[d, :, 0:256] = a
         p_send[d, :, 256:512] = b
@@ -158,7 +229,7 @@
     @pl.loop(1, F)
     def _(o):
         s = source_of(f, o)
-        remote(winp.at[s], w_recv.at[s], w_s.at[s], w_r.at[s], (f, r)).wait_recv()
+        remote(w_send.at[s], w_recv.at[s], w_s.at[s], w_r.at[s], (f, r)).wait_recv()
 
     w32[...] = w_recv[...].astype(F32)
     lane = lax.broadcasted_iota(jnp.int32, (F, 128), 1)
@@ -184,16 +255,18 @@
     prior_i = [jnp.concatenate([moved[2 * k], moved[2 * k + 1]], axis=1) for k in range(3)]
     prior_g = [moved[6], pltpu.roll(moved[6], 64, 1), moved[7]]
 
-    @pl.loop(1, F)
-    def _(o):
-        s = source_of(f, o)
+    @pl.loop(0, F - 1)
+    def _(i):
+        s = source_of(f, order(i))
         remote(p_send.at[s], p_recv.at[s], p_s.at[s], p_r.at[s], (f, r)).wait_recv()
         acc[...] += p_recv[s].astype(F32)
 
     raw = acc[...].astype(BF16)
-    win_i[...] = raw[SLOTS:, 0:256]
-    win_g[...] = raw[SLOTS:, 512:640]
     raw = raw.astype(F32)
+    for t in range(1, NSTEP):
+        rows = slice(SLOTS * t, SLOTS * (t + 1))
+        win_i[t - 1] = raw[rows, 0:256].astype(BF16)
+        win_g[t - 1] = raw[rows, 512:576].astype(BF16)
 
     def conv(prior, fresh, taps, bias):
         steps = prior + [fresh[SLOTS * t : SLOTS * (t + 1)] for t in range(NSTEP)]
@@ -206,7 +279,7 @@
         return got
 
     group = jnp.concatenate(
-        conv(prior_g, raw[:, 512:640], [par[9 + k : 10 + k, 0:128] for k in range(4)], par[13:14, 0:128]),
+        conv(prior_g, raw[:, 512:640], [gpar[k : k + 1] for k in range(4)], gpar[4:5]),
         axis=0,
     )
     gc_send[...] = jnp.where(half == 1, pltpu.roll(group, 64, 1), group).astype(BF16)
@@ -225,7 +298,7 @@
         def _():
             gc_recv[piece] = gc_send[...]
 
-    xs = conv(prior_i, raw[:, 0:256], [par[k : k + 1] for k in range(4)], par[4:5])
+    xs = conv(prior_i, raw[:, 0:256], [fi[k : k + 1] for k in range(4)], fib[...])
     step_raw = jnp.concatenate(
         [
             jnp.broadcast_to(raw[:, 576:577], (NSTEP * SLOTS, 128)),
@@ -233,9 +306,15 @@
         ],
         axis=1,
     )
-    v = step_raw + par[7:8]
+    for load in loads[15:]:
+        load.wait()
+
+    def head_row(values):
+        return jnp.where(lax.broadcasted_iota(jnp.int32, (1, 256), 1) < 128, values[0], values[1])
+
+    v = step_raw + head_row(sb)
     dt = jnp.maximum(v, 0.0) + jnp.log1p(jnp.exp(-jnp.abs(v)))
-    dec = jnp.exp(-dt * par[8:9])
+    dec = jnp.exp(-dt * head_row(dr))
     dts = [dt[SLOTS * t : SLOTS * (t + 1)] for t in range(NSTEP)]
     decs = [dec[SLOTS * t : SLOTS * (t + 1)] for t in range(NSTEP)]
 
@@ -297,13 +376,13 @@
                 term = term * grown
             total = term if total is None else total + term
             grown = decs[s] if grown is None else grown * decs[s]
-        total = total + grown * yk[:, t, :] + par[6:7] * xs[t]
+        total = total + grown * yk[:, t, :] + head_row(sg) * xs[t]
         gated.append(total * gates[SLOTS * t : SLOTS * (t + 1)])
     ga_all[f] = jnp.concatenate(gated, axis=0).astype(BF16)
 
-    @pl.loop(1, F)
-    def _(o):
-        d = peer_of(f, o)
+    @pl.loop(0, F - 1)
+    def _(i):
+        d = peer_of(f, order(i))
         remote(ga_all.at[f], ga_all.at[f], ga_s.at[d], ga_r.at[f], (d, r)).start()
 
     @pl.loop(0, SLOTS)
@@ -329,7 +408,7 @@
     def project_out(d):
         g = ga_all[d].astype(F32)
         squares = jnp.sum(g * g, axis=1, keepdims=True)
-        part = dot((g * par[5:6]).astype(BF16), wo[...], ((1,), (0,))).astype(BF16)
+        part = dot((g * gain[...]).astype(BF16), wo[...], ((1,), (0,))).astype(BF16)
         where = lax.broadcasted_iota(jnp.int32, (16, 128), 1)
         high = squares.astype(BF16).astype(F32)
         low = squares - high
@@ -355,9 +434,9 @@
 
     project_out(f)
 
-    @pl.loop(1, F)
-    def _(o):
-        s = source_of(f, o)
+    @pl.loop(0, F - 1)
+    def _(i):
+        s = source_of(f, order(i))
         remote(ga_all.at[s], ga_all.at[s], ga_s.at[s], ga_r.at[s], (f, r)).wait_recv()
         project_out(s)
 
@@ -424,7 +503,7 @@
     @pl.loop(1, F)
     def _(o):
         d = peer_of(f, o)
-        remote(winp.at[d], w_recv.at[f], w_s.at[d], w_r.at[f], (f, r)).wait_send()
+        remote(w_send.at[d], w_recv.at[f], w_s.at[d], w_r.at[f], (f, r)).wait_send()
         rows = pl.ds(2 * d, 2)
         remote(st_send.at[rows], st_recv.at[rows], st_s.at[d], st_r.at[f], (f, r)).wait_send()
         remote(p_send.at[d], p_recv.at[f], p_s.at[d], p_r.at[f], (f, r)).wait_send()
@@ -437,21 +516,28 @@
             remote(gc_send, gc_recv.at[piece], gc_s.at[m], gc_r.at[piece], (f, r)).wait_send()
 
 
-def mixer(idx, hid, wi, wg, wgs, wo, par, winp, state):
+def mixer(*operands):
     vmem = pl.BlockSpec(memory_space=pltpu.VMEM)
     dma = pltpu.SemaphoreType.DMA
     pairs = [2, R, F, F, F, 8, F, R, 2]
+    held = [(pltpu.SMEM if x.ndim == 1 else pltpu.VMEM)(x.shape, x.dtype) for x in operands[:-1]]
     return pl.pallas_call(
         kernel,
         out_shape=(
             jax.ShapeDtypeStruct((64, 128), BF16),
             jax.ShapeDtypeStruct((SLOTS, 256, 256), BF16),
-            jax.ShapeDtypeStruct((48, 256), BF16),
-            jax.ShapeDtypeStruct((48, 128), BF16),
+            jax.ShapeDtypeStruct((3, SLOTS, 256), BF16),
+            jax.ShapeDtypeStruct((3, SLOTS, 64), BF16),
         ),
-        in_specs=[pl.BlockSpec(memory_space=pltpu.SMEM)] + [vmem] * 7 + [pl.BlockSpec(memory_space=pl.ANY)],
+        in_specs=[pl.BlockSpec(memory_space=pl.ANY)] * len(operands),
         out_specs=(vmem,) * 4,
-        scratch_shapes=[
+        scratch_shapes=held
+        + [
+            pltpu.VMEM((128, 256), BF16),
+            pltpu.VMEM((8, 128), F32),
+            pltpu.VMEM((SLOTS, 8, 128), F32),
+            pltpu.VMEM((F, 16, 128), BF16),
+            pltpu.VMEM((3, SLOTS, 128), F32),
             pltpu.VMEM((R, 2, 32, 128), BF16),
             pltpu.VMEM((F, 64, 640), BF16),
             pltpu.VMEM((F, 64, 640), BF16),
@@ -476,12 +562,12 @@
             pltpu.SMEM((SLOTS,), jnp.int32),
         ]
         + [dma((n,)) for n in pairs for _ in range(2)]
-        + [dma((1,))],
+        + [dma((len(operands),))],
         compiler_params=pltpu.CompilerParams(
-            collective_id=0, has_side_effects=True, vmem_limit_bytes=48 * 2**20
+            collective_id=0, has_side_effects=True, vmem_limit_bytes=60 * 2**20
         ),
         name="mixer",
-    )(idx, hid, wi, wg, wgs, wo, par, winp, state)
+    )(*operands)
 
 
 def on_device(
@@ -506,59 +592,33 @@
     target_device,
     target_slot,
 ):
-    slot = jnp.arange(SLOTS, dtype=jnp.int32)
-    device = jnp.arange(F, dtype=jnp.int32)
-    match = (slot < live_counts[0])[:, None] & (target_device[:, None] == device[None, :])
-    earlier = jnp.sum(
-        (match[:, None, :] & (slot[:, None] < slot[None, :])[:, :, None]).astype(jnp.int32), axis=0
-    )
-    chosen = match[:, :, None] & (earlier[:, :, None] == jnp.arange(2, dtype=jnp.int32))
-    picker = chosen.reshape(SLOTS, 2 * F)
-    idx = jnp.sum(jnp.where(picker, slot[:, None], 0), axis=0)
-    sent_slot = jnp.sum(jnp.where(picker, target_slot[:, None] + 1, 0), axis=0) - 1
-    flat = jnp.concatenate(
-        [filter_inner_state.reshape(SLOTS, 768), filter_group_state.reshape(SLOTS, 192)], axis=1
-    )
-    packed = lax.dot_general(
-        picker.astype(BF16), flat, (((0,), (0,)), ((), ())), preferred_element_type=F32
-    ).astype(BF16)
-    slot_columns = jnp.broadcast_to(sent_slot[:, None], (2 * F, 64)).astype(BF16)
-    winp = jnp.concatenate([packed, slot_columns], axis=1).reshape(F, 16, 128)
-
-    def head_row(values):
-        return jnp.repeat(values, 128).reshape(1, 256)
-
-    par = jnp.concatenate(
-        [
-            filter_inner,
-            filter_inner_bias.reshape(1, 256),
-            norm_gain.reshape(1, 256),
-            head_row(skip_gain),
-            head_row(step_bias),
-            head_row(decay_rate),
-            jnp.pad(filter_group, ((0, 0), (0, 192))),
-            jnp.pad(filter_group_bias.reshape(1, 64), ((0, 0), (0, 192))),
-            jnp.zeros((2, 256), F32),
-        ],
-        axis=0,
-    )
-    wgs = jnp.concatenate([group_weight, step_weight, jnp.zeros((256, 62), BF16)], axis=1)
     out, new_state, win_i, win_g = mixer(
-        idx,
+        live_counts,
+        target_device,
+        target_slot,
+        step_bias,
+        decay_rate,
+        skip_gain,
         hidden.reshape(64, 128),
         inner_weight,
         gate_weight,
-        wgs,
+        group_weight.T,
+        step_weight.T,
         output_weight,
-        par,
-        winp,
+        filter_inner,
+        filter_inner_bias.reshape(1, 256),
+        filter_group,
+        filter_group_bias.reshape(1, 64),
+        norm_gain.reshape(1, 256),
+        jnp.transpose(filter_inner_state, (1, 0, 2)),
+        jnp.transpose(filter_group_state, (1, 0, 2)),
         recurrent_state.reshape(SLOTS, 256, 256),
     )
     return (
         out.reshape(NSTEP, SLOTS, 128),
         new_state.reshape(SLOTS, 2, 128, 256),
-        jnp.transpose(win_i.reshape(3, SLOTS, 256), (1, 0, 2)),
-        jnp.transpose(win_g[:, 0:64].reshape(3, SLOTS, 64), (1, 0, 2)),
+        jnp.transpose(win_i, (1, 0, 2)),
+        jnp.transpose(win_g, (1, 0, 2)),
     )
 
 

time: 321 us -> 256 us (0.80)
  the two profiles are of different devices: /device:TPU:63 before, /device:TPU:41 now
where the time goes in v2:
time: 256 us; the launch traced here: 255 us
  Pallas kernels  248 us (97%)
  local copies, waits for them, and re-layouts  5.68 us (2%)
    pallas_call x1, Pallas kernels, mixer(): pl.pallas_call(kernel, out_shape=(jax.ShapeDtypeStruct((64, 128), BF16),...  248 us
    unnamed x8, local copies, waits for them, and re-layouts  5.68 us

profile of v2, /device:TPU:41, one launch (start us, length us, event | category | flops | bytes accessed | tf_op | source)
XLA Modules:
  0.0 255.3 jit_solution(5583041617776826512)
XLA Ops:
  1.3 248.3 %mixer.1 = (bf16[64,128]{1,0:T(8,128)(2,1)}, bf16[16,256,256]{2,1,0:T(8,128)(2,1)}, bf16[3,16,256]{2,1,0:T(8,128)(2,1)}, bf16[3,16,64]{2,1,0:T(8,128)(2,1)}) custom-call(s32[1]{0:T(128)S(6)} %copy.28.live_h, s32[16]{0:T(128)} %td_h.1, s32[16]{0:T(128)} %ts_h.1, f32[2]{0:T(128)} %sb_h.1, f32[2]{0:T(128)} %dr_h.1, f32[2]{0:T(128)} %sg_h.1, ...), custom_call_target="tpu_custom_call" | custom-call | tf_op jit(solution)/shard_map/mixer/pallas_call | solution.py:524
  249.6 1.3 copy.29
  251.0 0.0 copy-start
  251.0 0.0 copy-start.1
  251.0 3.1 %copy.30 = bf16[16,2,128,256]{3,2,1,0:T(8,128)(2,1)} copy(bf16[16,2,128,256]{3,2,1,0:T(8,128)(2,1)} %bitcast.14) | data formatting | bytes 4194304
  254.1 0.0 copy-done
  254.1 0.6 copy.31
  254.7 0.0 copy-done.1
  254.7 0.6 copy.32
Async XLA Ops:
  251.0 3.1 %copy-start = (bf16[3,16,256]{2,1,0:T(8,128)(2,1)S(1)}, bf16[3,16,256]{2,1,0:T(8,128)(2,1)}, u32[]{:S(2)}) copy-start(bf16[3,16,256]{2,1,0:T(8,128)(2,1)} %get-tuple-element.10) | copy-start | bytes 73732
  251.0 3.8 %copy-start.1 = (bf16[3,16,64]{2,1,0:T(8,128)(2,1)S(1)}, bf16[3,16,64]{2,1,0:T(8,128)(2,1)}, u32[]{:S(2)}) copy-start(bf16[3,16,64]{2,1,0:T(8,128)(2,1)} %get-tuple-element.11) | copy-start | bytes 18436

commit v3 on v2

--- a/solution.py
+++ b/solution.py
@@ -13,7 +13,11 @@
 NSTEP = 4
 SLOTS = 16
 EPS = 1e-05
-EARLY = 4
+ALONG = (1, 7, 2, 6, 3, 5, 4)
+ACROSS = (4, 3, 5, 2, 6, 1, 7, 0)
+CROSS_ROWS = (0, 16, 0)
+ALONG_ROWS = (0, 14, 0)
+PASS_ROWS = (0, 14, 0)
 F32 = jnp.float32
 BF16 = jnp.bfloat16
 
@@ -47,8 +51,8 @@
     live, td, ts, sb, dr, sg, hid, wi, wg, wgr, wst, wo, fi, fib, fg, fgb, gain, wini, wing,
     wgs, gpar, win32, w_send, wg32,
     hid_all, p_send, p_recv, w_recv, w32, st_v, st_send, st_recv, gc_send, gc_recv,
-    ga_all, po_send, po_recv, fin_send, fin_recv, acc, ck, bk, uk, yk, ssum, jq,
-    h1_s, h1_r, h2_s, h2_r, w_s, w_r, st_s, st_r, p_s, p_r, gc_s, gc_r, ga_s, ga_r, po_s, po_r, fin_s, fin_r, loc,
+    ga_all, po_send, po_recv, fin_send, fin_recv, acc, ck, bk, uk, yk, ssum, jq, pick, relay, py_send, py_recv,
+    h1_s, h1_r, h2_s, h2_r, w_s, w_r, st_s, st_r, p_s, p_r, gc_s, gc_r, ga_s, ga_r, po_s, po_r, fin_s, fin_r, rl_s, rl_r, py_s, py_r, gf_s, gf_r, loc,
 ):
     f = lax.axis_index("fsdp")
     r = lax.axis_index("roll")
@@ -123,6 +127,8 @@
     @pl.loop(0, F)
     def _(d):
         got, to = picks(d)
+        for c in range(2):
+            pick[2 * d + c] = got[c]
         w_send[d] = jnp.concatenate(
             [
                 jnp.where((row8 == 7) & (lane8 >= 64), to[c].astype(F32), win32[got[c]])
@@ -131,6 +137,43 @@
             axis=0,
         ).astype(BF16)
 
+    loads[4].wait()
+
+    @pl.loop(0, 2 * F)
+    def _(j):
+        st_send[j] = st_v[pick[j]]
+
+    for c in range(2):
+        st_recv[2 * f + c] = st_send[2 * f + c]
+
+    fy, fz = f // Z, f % Z
+    over = (1 - fy) * Z + fz
+
+    def turn(b):
+        return (fz + jnp.where(half == 0, b, (Z - b) % Z)) % Z
+
+    def upto(rows, point):
+        return range(sum(rows[:point]), sum(rows[: point + 1]))
+
+    def send_rows(point):
+        for k in upto(CROSS_ROWS, point):
+            c = k % 2
+            z = turn(ACROSS[k // 2])
+            at = 2 * ((1 - fy) * Z + z) + c
+            if ACROSS[k // 2]:
+                remote(st_send.at[at], relay.at[2 * z + c], st_s.at[at], rl_r.at[2 * z + c], (over, r)).start()
+            else:
+                remote(st_send.at[at], st_recv.at[2 * f + c], st_s.at[at], st_r.at[2 * f + c], (over, r)).start()
+        for k in upto(ALONG_ROWS, point):
+            d = fy * Z + turn(ALONG[k // 2])
+            at, to = 2 * d + k % 2, 2 * f + k % 2
+            remote(st_send.at[at], st_recv.at[to], st_s.at[at], st_r.at[to], (d, r)).start()
+        for k in upto(PASS_ROWS, point):
+            z = turn(ACROSS[k // 2])
+            at, to = 2 * z + k % 2, 2 * over + k % 2
+            remote(relay.at[at], relay.at[at], rl_s.at[at], rl_r.at[at], (f, r)).wait_recv()
+            remote(relay.at[at], st_recv.at[to], rl_s.at[at], st_r.at[to], (fy * Z + z, r)).start()
+
     loads[0].wait()
     pl.semaphore_wait(barrier, F - 1 + R - 1 + jnp.where(home != f, 2, 0))
 
@@ -154,20 +197,7 @@
 
     w_recv[f] = w_send[f]
 
-    loads[4].wait()
-
-    def send_states(i):
-        d = peer_of(f, order(i))
-        got, _ = picks(d)
-        for c in range(2):
-            st_send[2 * d + c] = st_v[got[c]]
-        remote(
-            st_send.at[pl.ds(2 * d, 2)], st_recv.at[pl.ds(2 * f, 2)], st_s.at[d], st_r.at[f], (d, r)
-        ).start()
-
-    @pl.loop(0, EARLY)
-    def _(i):
-        send_states(i)
+    send_rows(0)
 
     for k in range(2):
 
@@ -180,17 +210,11 @@
         to = (r + o) % R
         remote(hid_all.at[r], hid_all.at[r], h2_s.at[to], h2_r.at[r], (f, to)).start()
 
-    @pl.loop(EARLY, F - 1)
-    def _(i):
-        send_states(i)
-
-    got, _ = picks(f)
-    for c in range(2):
-        st_recv[2 * f + c] = st_v[got[c]]
-
-    def project(d):
-        for h in range(2):
-            chunk = 2 * d + h
+    send_rows(1)
+
+    def project(z):
+        chunks = [2 * (y * Z + z) + h for y in range(2) for h in range(2)]
+        for chunk in chunks:
 
             @pl.when(chunk != r)
             def _():
@@ -199,32 +223,37 @@
                 ).wait_recv()
 
         rows = jnp.concatenate(
-            [
-                jnp.concatenate([hid_all[2 * d + h, 0], hid_all[2 * d + h, 1]], axis=1)
-                for h in range(2)
-            ],
+            [jnp.concatenate([hid_all[chunk, 0], hid_all[chunk, 1]], axis=1) for chunk in chunks],
             axis=0,
         )
         nn = ((1,), (0,))
         return (
-            dot(rows, wi[...], nn).astype(BF16),
-            dot(rows, wg[...], nn).astype(BF16),
-            dot(rows, wgs[...], ((1,), (1,))).astype(BF16),
+            dot(rows, wi[...], nn),
+            dot(rows, wg[...], nn),
+            dot(rows, wgs[...], ((1,), (1,))),
         )
 
-    @pl.loop(0, F - 1)
+    def along(i):
+        return (fz + jnp.where(i % 2 == half, i // 2 + 1, Z - 1 - i // 2)) % Z
+
+    @pl.loop(0, Z - 1)
     def _(i):
-        d = peer_of(f, order(i))
-        a, b, c = project(d)
-        p_send[d, :, 0:256] = a
-        p_send[d, :, 256:512] = b
-        p_send[d, :, 512:640] = c
-        remote(p_send.at[d], p_recv.at[f], p_s.at[d], p_r.at[f], (d, r)).start()
-
-    a, b, c = project(f)
-    acc[:, 0:256] = a.astype(F32)
-    acc[:, 256:512] = b.astype(F32)
-    acc[:, 512:640] = c.astype(F32)
+        z = along(i)
+        parts = project(z)
+        for y in range(2):
+            rows = slice(64 * y, 64 * y + 64)
+            p_send[z, y, :, 0:256] = parts[0][rows].astype(BF16)
+            p_send[z, y, :, 256:512] = parts[1][rows].astype(BF16)
+            p_send[z, y, :, 512:640] = parts[2][rows].astype(BF16)
+        remote(p_send.at[z], p_recv.at[fz], p_s.at[z], p_r.at[fz], (fy * Z + z, r)).start()
+
+    send_rows(2)
+    parts = project(fz)
+    for y in range(2):
+        rows = slice(64 * y, 64 * y + 64)
+        acc[y, :, 0:256] = parts[0][rows]
+        acc[y, :, 256:512] = parts[1][rows]
+        acc[y, :, 512:640] = parts[2][rows]
 
     @pl.loop(1, F)
     def _(o):
@@ -255,13 +284,22 @@
     prior_i = [jnp.concatenate([moved[2 * k], moved[2 * k + 1]], axis=1) for k in range(3)]
     prior_g = [moved[6], pltpu.roll(moved[6], 64, 1), moved[7]]
 
-    @pl.loop(0, F - 1)
+    @pl.loop(0, Z - 1)
     def _(i):
-        s = source_of(f, order(i))
-        remote(p_send.at[s], p_recv.at[s], p_s.at[s], p_r.at[s], (f, r)).wait_recv()
-        acc[...] += p_recv[s].astype(F32)
-
-    raw = acc[...].astype(BF16)
+        z = along(i)
+        remote(p_send.at[z], p_recv.at[z], p_s.at[z], p_r.at[z], (f, r)).wait_recv()
+        acc[1 - fy] += p_recv[z, 1 - fy].astype(F32)
+
+    py_send[...] = acc[1 - fy].astype(BF16)
+    across = remote(py_send, py_recv, py_s.at[0], py_r.at[0], (over, r))
+    across.start()
+
+    @pl.loop(0, Z - 1)
+    def _(i):
+        acc[fy] += p_recv[along(i), fy].astype(F32)
+
+    across.wait_recv()
+    raw = (acc[fy] + py_recv[...].astype(F32)).astype(BF16)
     raw = raw.astype(F32)
     for t in range(1, NSTEP):
         rows = slice(SLOTS * t, SLOTS * (t + 1))
@@ -351,21 +389,8 @@
         tail = decs[t] if tail is None else decs[t] * tail
     uk[:, 4, :] = tail
 
-    @pl.loop(1, F)
-    def _(o):
-        s = source_of(f, o)
-        rows = pl.ds(2 * s, 2)
-        remote(st_send.at[rows], st_recv.at[rows], st_s.at[s], st_r.at[s], (f, r)).wait_recv()
-
-    @pl.loop(0, SLOTS)
-    def _(q):
-        j = jq[q]
-        start = st_recv[jnp.clip(j, 0, 2 * F - 1)]
-        y = dot(ck[q].astype(BF16), start, ((1,), (1,)))
-        yk[q] = jnp.where(j >= 0, y, 0.0)
-
     gates = silu(raw[:, 256:512])
-    gated = []
+    fresh = []
     for t in range(NSTEP):
         total = None
         grown = None
@@ -376,14 +401,41 @@
                 term = term * grown
             total = term if total is None else total + term
             grown = decs[s] if grown is None else grown * decs[s]
-        total = total + grown * yk[:, t, :] + head_row(sg) * xs[t]
-        gated.append(total * gates[SLOTS * t : SLOTS * (t + 1)])
+        fresh.append((total + head_row(sg) * xs[t], grown))
+
+    @pl.loop(1, F)
+    def _(o):
+        s = source_of(f, o)
+        for c in range(2):
+            at = 2 * s + c
+            remote(st_send.at[at], st_recv.at[at], st_s.at[at], st_r.at[at], (f, r)).wait_recv()
+
+    @pl.loop(0, SLOTS)
+    def _(q):
+        j = jq[q]
+        y = dot(ck[q].astype(BF16), st_recv[jnp.clip(j, 0, 2 * F - 1)], ((1,), (1,)))
+        yk[q] = jnp.where(j >= 0, y, 0.0)
+
+    gated = [
+        (fresh[t][0] + fresh[t][1] * yk[:, t, :]) * gates[SLOTS * t : SLOTS * (t + 1)]
+        for t in range(NSTEP)
+    ]
     ga_all[f] = jnp.concatenate(gated, axis=0).astype(BF16)
 
-    @pl.loop(0, F - 1)
-    def _(i):
-        d = peer_of(f, order(i))
-        remote(ga_all.at[f], ga_all.at[f], ga_s.at[d], ga_r.at[f], (d, r)).start()
+    remote(ga_all.at[f], ga_all.at[f], ga_s.at[over], ga_r.at[f], (over, r)).start()
+
+    def spread(block, sems):
+        @pl.loop(0, Z - 1)
+        def _(i):
+            d = fy * Z + along(i)
+            remote(ga_all.at[block], ga_all.at[block], sems.at[d], ga_r.at[block], (d, r)).start()
+
+    def arrived(block):
+        remote(ga_all.at[block], ga_all.at[block], ga_s.at[block], ga_r.at[block], (f, r)).wait_recv()
+
+    spread(f, ga_s)
+    arrived(over)
+    spread(over, gf_s)
 
     @pl.loop(0, SLOTS)
     def _(q):
@@ -405,6 +457,7 @@
             factor = jnp.concatenate([rate[:, rows], rate[:, rows]], axis=1)
             new_state[q, rows, :] = (start[rows] * factor + added[rows]).astype(BF16)
 
+
     def project_out(d):
         g = ga_all[d].astype(F32)
         squares = jnp.sum(g * g, axis=1, keepdims=True)
@@ -433,18 +486,21 @@
                 po_recv[r] = po_send[r]
 
     project_out(f)
-
-    @pl.loop(0, F - 1)
-    def _(i):
-        s = source_of(f, order(i))
-        remote(ga_all.at[s], ga_all.at[s], ga_s.at[s], ga_r.at[s], (f, r)).wait_recv()
-        project_out(s)
-
-    acc[0:32, 0:256] = jnp.zeros((32, 256), F32)
+    project_out(over)
+    for y in range(2):
+
+        @pl.loop(0, Z - 1)
+        def _(i):
+            block = jnp.where(y == 0, fy, 1 - fy) * Z + along(i)
+            arrived(block)
+            project_out(block)
+
+
+    acc[0, 0:32, 0:256] = jnp.zeros((32, 256), F32)
 
     @pl.loop(0, 4)
     def _(g):
-        acc[32:64, 0:256] = jnp.zeros((32, 256), F32)
+        acc[0, 32:64, 0:256] = jnp.zeros((32, 256), F32)
         ssum[...] = jnp.zeros((16, 128), F32)
 
         @pl.loop(0, 8)
@@ -455,8 +511,8 @@
             def _():
                 remote(po_send.at[s], po_recv.at[s], po_s.at[s], po_r.at[s], (f, r)).wait_recv()
 
-            acc[32:64, 0:128] += po_recv[s, 0:32, :].astype(F32)
-            acc[32:64, 128:256] += po_recv[s, 32:64, :].astype(F32)
+            acc[0, 32:64, 0:128] += po_recv[s, 0:32, :].astype(F32)
+            acc[0, 32:64, 128:256] += po_recv[s, 32:64, :].astype(F32)
             ssum[...] += po_recv[s, 64:80, :].astype(F32)
 
         squares = ssum[...]
@@ -464,10 +520,10 @@
             [squares[:, 0:1] + squares[:, 32:33], squares[:, 64:65] + squares[:, 96:97]], axis=0
         )
         scale = lax.rsqrt(squares / (HPG * 128) + EPS)
-        acc[0:32, 0:256] += acc[32:64, 0:256] * scale
+        acc[0, 0:32, 0:256] += acc[0, 32:64, 0:256] * scale
 
     for k in range(2):
-        fin_send[k] = acc[0:32, 128 * k : 128 * k + 128].astype(BF16)
+        fin_send[k] = acc[0, 0:32, 128 * k : 128 * k + 128].astype(BF16)
 
         @pl.when(jnp.logical_not(is_self(k)))
         def _():
@@ -478,6 +534,7 @@
         @pl.when(is_self(k))
         def _():
             fin_recv[k] = fin_send[k]
+
 
     for k in range(2):
 
@@ -504,10 +561,23 @@
     def _(o):
         d = peer_of(f, o)
         remote(w_send.at[d], w_recv.at[f], w_s.at[d], w_r.at[f], (f, r)).wait_send()
-        rows = pl.ds(2 * d, 2)
-        remote(st_send.at[rows], st_recv.at[rows], st_s.at[d], st_r.at[f], (f, r)).wait_send()
-        remote(p_send.at[d], p_recv.at[f], p_s.at[d], p_r.at[f], (f, r)).wait_send()
+        for c in range(2):
+            at = 2 * d + c
+            remote(st_send.at[at], st_recv.at[at], st_s.at[at], st_r.at[at], (f, r)).wait_send()
+
+    across.wait_send()
+    remote(ga_all.at[f], ga_all.at[f], ga_s.at[over], ga_r.at[f], (f, r)).wait_send()
+
+    @pl.loop(0, Z - 1)
+    def _(i):
+        z = along(i)
+        d = fy * Z + z
+        remote(p_send.at[z], p_recv.at[fz], p_s.at[z], p_r.at[fz], (f, r)).wait_send()
         remote(ga_all.at[f], ga_all.at[f], ga_s.at[d], ga_r.at[f], (f, r)).wait_send()
+        remote(ga_all.at[over], ga_all.at[over], gf_s.at[d], ga_r.at[over], (f, r)).wait_send()
+        for c in range(2):
+            at = 2 * z + c
+            remote(relay.at[at], relay.at[at], rl_s.at[at], rl_r.at[at], (f, r)).wait_send()
 
     @pl.loop(0, 8)
     def _(m):
@@ -519,7 +589,7 @@
 def mixer(*operands):
     vmem = pl.BlockSpec(memory_space=pltpu.VMEM)
     dma = pltpu.SemaphoreType.DMA
-    pairs = [2, R, F, F, F, 8, F, R, 2]
+    pairs = [2, R, F, 2 * F, F, 8, F, R, 2, F, 1, F]
     held = [(pltpu.SMEM if x.ndim == 1 else pltpu.VMEM)(x.shape, x.dtype) for x in operands[:-1]]
     return pl.pallas_call(
         kernel,
@@ -539,8 +609,8 @@
             pltpu.VMEM((F, 16, 128), BF16),
             pltpu.VMEM((3, SLOTS, 128), F32),
             pltpu.VMEM((R, 2, 32, 128), BF16),
-            pltpu.VMEM((F, 64, 640), BF16),
-            pltpu.VMEM((F, 64, 640), BF16),
+            pltpu.VMEM((Z, 2, 64, 640), BF16),
+            pltpu.VMEM((Z, 2, 64, 640), BF16),
             pltpu.VMEM((F, 16, 128), BF16),
             pltpu.VMEM((F, 16, 128), F32),
             pltpu.VMEM((SLOTS, 256, 256), BF16),
@@ -553,13 +623,17 @@
             pltpu.VMEM((R, 80, 128), BF16),
             pltpu.VMEM((2, 32, 128), BF16),
             pltpu.VMEM((2, 32, 128), BF16),
-            pltpu.VMEM((64, 640), F32),
+            pltpu.VMEM((2, 64, 640), F32),
             pltpu.VMEM((SLOTS, 8, 256), F32),
             pltpu.VMEM((SLOTS, 8, 256), F32),
             pltpu.VMEM((SLOTS, 8, 256), F32),
             pltpu.VMEM((SLOTS, 8, 256), F32),
             pltpu.VMEM((16, 128), F32),
             pltpu.SMEM((SLOTS,), jnp.int32),
+            pltpu.SMEM((2 * F,), jnp.int32),
+            pltpu.VMEM((2 * Z, 256, 256), BF16),
+            pltpu.VMEM((64, 640), BF16),
+            pltpu.VMEM((64, 640), BF16),
         ]
         + [dma((n,)) for n in pairs for _ in range(2)]
         + [dma((len(operands),))],

time: 256 us -> 215 us (0.84)
  Pallas kernels: 248 us -> 208 us
    pallas_call x1, Pallas kernels: 248 us -> 208 us  [mixer(): pl.pallas_call(kernel, out_shape=(jax.ShapeDtypeStruct((64, 128), BF16),...]
where the time goes in v3:
time: 215 us
  Pallas kernels  208 us (97%)
  local copies, waits for them, and re-layouts  5.68 us (3%)
    pallas_call x1, Pallas kernels, mixer(): pl.pallas_call(kernel, out_shape=(jax.ShapeDtypeStruct((64, 128), BF16),...  208 us
    unnamed x8, local copies, waits for them, and re-layouts  5.68 us

profile of v3, /device:TPU:41, one launch (start us, length us, event | category | flops | bytes accessed | tf_op | source)
XLA Modules:
  0.0 214.6 jit_solution(11581615232511073569)
XLA Ops:
  1.3 207.7 %mixer.1 = (bf16[64,128]{1,0:T(8,128)(2,1)}, bf16[16,256,256]{2,1,0:T(8,128)(2,1)}, bf16[3,16,256]{2,1,0:T(8,128)(2,1)}, bf16[3,16,64]{2,1,0:T(8,128)(2,1)}) custom-call(s32[1]{0:T(128)S(6)} %copy.28.live_h, s32[16]{0:T(128)} %td_h.1, s32[16]{0:T(128)} %ts_h.1, f32[2]{0:T(128)} %sb_h.1, f32[2]{0:T(128)} %dr_h.1, f32[2]{0:T(128)} %sg_h.1, ...), custom_call_target="tpu_custom_call" | custom-call | tf_op jit(solution)/shard_map/mixer/pallas_call | solution.py:594
  209.0 1.3 copy.29
  210.3 0.0 copy-start
  210.3 0.0 copy-start.1
  210.3 3.1 %copy.30 = bf16[16,2,128,256]{3,2,1,0:T(8,128)(2,1)} copy(bf16[16,2,128,256]{3,2,1,0:T(8,128)(2,1)} %bitcast.14) | data formatting | bytes 4194304
  213.4 0.0 copy-done
  213.4 0.6 copy.31
  214.0 0.0 copy-done.1
  214.0 0.6 copy.32
Async XLA Ops:
  210.3 3.1 %copy-start = (bf16[3,16,256]{2,1,0:T(8,128)(2,1)S(1)}, bf16[3,16,256]{2,1,0:T(8,128)(2,1)}, u32[]{:S(2)}) copy-start(bf16[3,16,256]{2,1,0:T(8,128)(2,1)} %get-tuple-element.10) | copy-start | bytes 73732
  210.3 3.8 %copy-start.1 = (bf16[3,16,64]{2,1,0:T(8,128)(2,1)S(1)}, bf16[3,16,64]{2,1,0:T(8,128)(2,1)}, u32[]{:S(2)}) copy-start(bf16[3,16,64]{2,1,0:T(8,128)(2,1)} %get-tuple-element.11) | copy-start | bytes 18436

commit v4 on v3

--- a/solution.py
+++ b/solution.py
@@ -51,8 +51,8 @@
     live, td, ts, sb, dr, sg, hid, wi, wg, wgr, wst, wo, fi, fib, fg, fgb, gain, wini, wing,
     wgs, gpar, win32, w_send, wg32,
     hid_all, p_send, p_recv, w_recv, w32, st_v, st_send, st_recv, gc_send, gc_recv,
-    ga_all, po_send, po_recv, fin_send, fin_recv, acc, ck, bk, uk, yk, ssum, jq, pick, relay, py_send, py_recv,
-    h1_s, h1_r, h2_s, h2_r, w_s, w_r, st_s, st_r, p_s, p_r, gc_s, gc_r, ga_s, ga_r, po_s, po_r, fin_s, fin_r, rl_s, rl_r, py_s, py_r, gf_s, gf_r, loc,
+    ga_all, po_send, po_recv, fin_send, fin_recv, acc, ck, bk, uk, yk, ssum, jq, pick, relay, py_send, py_recv, ph_send, ph_recv,
+    h1_s, h1_r, h2_s, h2_r, w_s, w_r, st_s, st_r, p_s, p_r, gc_s, gc_r, ga_s, ga_r, po_s, po_r, fin_s, fin_r, rl_s, rl_r, py_s, py_r, gf_s, gf_r, ph_s, ph_r, loc,
 ):
     f = lax.axis_index("fsdp")
     r = lax.axis_index("roll")
@@ -458,6 +458,8 @@
             new_state[q, rows, :] = (start[rows] * factor + added[rows]).astype(BF16)
 
 
+    group_index, member = r // 8, r % 8
+
     def project_out(d):
         g = ga_all[d].astype(F32)
         squares = jnp.sum(g * g, axis=1, keepdims=True)
@@ -477,13 +479,16 @@
             po_send[chunk, 32:64, :] = part[at : at + 32, 128:256]
             po_send[chunk, 64:80, :] = squares_tile
 
-            @pl.when(chunk != r)
+            to = 8 * group_index + chunk % 8
+
+            @pl.when(to != r)
             def _():
-                remote(po_send.at[chunk], po_recv.at[r], po_s.at[chunk], po_r.at[r], (f, chunk)).start()
-
-            @pl.when(chunk == r)
+                slot = 4 * member + chunk // 8
+                remote(po_send.at[chunk], po_recv.at[slot], po_s.at[chunk], po_r.at[slot], (f, to)).start()
+
+            @pl.when(to == r)
             def _():
-                po_recv[r] = po_send[r]
+                po_recv[4 * member + chunk // 8] = po_send[chunk]
 
     project_out(f)
     project_out(over)
@@ -496,8 +501,6 @@
             project_out(block)
 
 
-    acc[0, 0:32, 0:256] = jnp.zeros((32, 256), F32)
-
     @pl.loop(0, 4)
     def _(g):
         acc[0, 32:64, 0:256] = jnp.zeros((32, 256), F32)
@@ -505,22 +508,45 @@
 
         @pl.loop(0, 8)
         def _(i):
-            s = 8 * g + i
-
-            @pl.when(s != r)
+            slot = 4 * i + g
+
+            @pl.when(i != member)
             def _():
-                remote(po_send.at[s], po_recv.at[s], po_s.at[s], po_r.at[s], (f, r)).wait_recv()
-
-            acc[0, 32:64, 0:128] += po_recv[s, 0:32, :].astype(F32)
-            acc[0, 32:64, 128:256] += po_recv[s, 32:64, :].astype(F32)
-            ssum[...] += po_recv[s, 64:80, :].astype(F32)
+                remote(po_send.at[slot], po_recv.at[slot], po_s.at[slot], po_r.at[slot], (f, r)).wait_recv()
+
+            acc[0, 32:64, 0:128] += po_recv[slot, 0:32, :].astype(F32)
+            acc[0, 32:64, 128:256] += po_recv[slot, 32:64, :].astype(F32)
+            ssum[...] += po_recv[slot, 64:80, :].astype(F32)
 
         squares = ssum[...]
         squares = jnp.concatenate(
             [squares[:, 0:1] + squares[:, 32:33], squares[:, 64:65] + squares[:, 96:97]], axis=0
         )
         scale = lax.rsqrt(squares / (HPG * 128) + EPS)
-        acc[0, 0:32, 0:256] += acc[0, 32:64, 0:256] * scale
+        scaled = (acc[0, 32:64, 0:256] * scale).astype(BF16)
+        ph_send[g, 0:32, :] = scaled[:, 0:128]
+        ph_send[g, 32:64, :] = scaled[:, 128:256]
+
+        @pl.when(g != group_index)
+        def _():
+            remote(
+                ph_send.at[g], ph_recv.at[group_index], ph_s.at[g], ph_r.at[group_index], (f, 8 * g + member)
+            ).start()
+
+        @pl.when(g == group_index)
+        def _():
+            ph_recv[g] = ph_send[g]
+
+    acc[0, 0:32, 0:256] = jnp.zeros((32, 256), F32)
+
+    @pl.loop(0, 4)
+    def _(g):
+        @pl.when(g != group_index)
+        def _():
+            remote(ph_send.at[g], ph_recv.at[g], ph_s.at[g], ph_r.at[g], (f, r)).wait_recv()
+
+        acc[0, 0:32, 0:128] += ph_recv[g, 0:32, :].astype(F32)
+        acc[0, 0:32, 128:256] += ph_recv[g, 32:64, :].astype(F32)
 
     for k in range(2):
         fin_send[k] = acc[0, 0:32, 128 * k : 128 * k + 128].astype(BF16)
@@ -555,7 +581,6 @@
     def _(o):
         to = (r + o) % R
         remote(hid_all.at[r], hid_all.at[r], h2_s.at[to], h2_r.at[r], (f, r)).wait_send()
-        remote(po_send.at[to], po_recv.at[r], po_s.at[to], po_r.at[r], (f, r)).wait_send()
 
     @pl.loop(1, F)
     def _(o):
@@ -564,6 +589,18 @@
         for c in range(2):
             at = 2 * d + c
             remote(st_send.at[at], st_recv.at[at], st_s.at[at], st_r.at[at], (f, r)).wait_send()
+
+    @pl.loop(0, R)
+    def _(chunk):
+        @pl.when(chunk % 8 != member)
+        def _():
+            remote(po_send.at[chunk], po_recv.at[chunk], po_s.at[chunk], po_r.at[chunk], (f, r)).wait_send()
+
+    @pl.loop(0, 4)
+    def _(g):
+        @pl.when(g != group_index)
+        def _():
+            remote(ph_send.at[g], ph_recv.at[g], ph_s.at[g], ph_r.at[g], (f, r)).wait_send()
 
     across.wait_send()
     remote(ga_all.at[f], ga_all.at[f], ga_s.at[over], ga_r.at[f], (f, r)).wait_send()
@@ -589,7 +626,7 @@
 def mixer(*operands):
     vmem = pl.BlockSpec(memory_space=pltpu.VMEM)
     dma = pltpu.SemaphoreType.DMA
-    pairs = [2, R, F, 2 * F, F, 8, F, R, 2, F, 1, F]
+    pairs = [2, R, F, 2 * F, F, 8, F, R, 2, F, 1, F, 4]
     held = [(pltpu.SMEM if x.ndim == 1 else pltpu.VMEM)(x.shape, x.dtype) for x in operands[:-1]]
     return pl.pallas_call(
         kernel,
@@ -634,6 +671,8 @@
             pltpu.VMEM((2 * Z, 256, 256), BF16),
             pltpu.VMEM((64, 640), BF16),
             pltpu.VMEM((64, 640), BF16),
+            pltpu.VMEM((4, 64, 128), BF16),
+            pltpu.VMEM((4, 64, 128), BF16),
         ]
         + [dma((n,)) for n in pairs for _ in range(2)]
         + [dma((len(operands),))],

time: 215 us -> 212 us (0.986)
  the two profiles are of different devices: /device:TPU:41 before, /device:TPU:23 now
where the time goes in v4:
time: 212 us; the launch traced here: 211 us
  Pallas kernels  204 us (96%)
  local copies, waits for them, and re-layouts  5.68 us (3%)
    pallas_call x1, Pallas kernels, mixer(): pl.pallas_call(kernel, out_shape=(jax.ShapeDtypeStruct((64, 128), BF16),...  204 us
    unnamed x8, local copies, waits for them, and re-layouts  5.68 us

profile of v4, /device:TPU:23, one launch (start us, length us, event | category | flops | bytes accessed | tf_op | source)
XLA Modules:
  0.0 211.5 jit_solution(11941369802293434534)
XLA Ops:
  1.3 204.5 %mixer.1 = (bf16[64,128]{1,0:T(8,128)(2,1)}, bf16[16,256,256]{2,1,0:T(8,128)(2,1)}, bf16[3,16,256]{2,1,0:T(8,128)(2,1)}, bf16[3,16,64]{2,1,0:T(8,128)(2,1)}) custom-call(s32[1]{0:T(128)S(6)} %copy.28.live_h, s32[16]{0:T(128)} %td_h.1, s32[16]{0:T(128)} %ts_h.1, f32[2]{0:T(128)} %sb_h.1, f32[2]{0:T(128)} %dr_h.1, f32[2]{0:T(128)} %sg_h.1, ...), custom_call_target="tpu_custom_call" | custom-call | tf_op jit(solution)/shard_map/mixer/pallas_call | solution.py:631
  205.8 1.3 copy.29
  207.1 0.0 copy-start
  207.1 0.0 copy-start.1
  207.1 3.1 %copy.30 = bf16[16,2,128,256]{3,2,1,0:T(8,128)(2,1)} copy(bf16[16,2,128,256]{3,2,1,0:T(8,128)(2,1)} %bitcast.14) | data formatting | bytes 4194304
  210.2 0.0 copy-done
  210.2 0.6 copy.31
  210.9 0.0 copy-done.1
  210.9 0.6 copy.32
Async XLA Ops:
  207.1 3.1 %copy-start = (bf16[3,16,256]{2,1,0:T(8,128)(2,1)S(1)}, bf16[3,16,256]{2,1,0:T(8,128)(2,1)}, u32[]{:S(2)}) copy-start(bf16[3,16,256]{2,1,0:T(8,128)(2,1)} %get-tuple-element.10) | copy-start | bytes 73732
  207.1 3.8 %copy-start.1 = (bf16[3,16,64]{2,1,0:T(8,128)(2,1)S(1)}, bf16[3,16,64]{2,1,0:T(8,128)(2,1)}, u32[]{:S(2)}) copy-start(bf16[3,16,64]{2,1,0:T(8,128)(2,1)} %get-tuple-element.11) | copy-start | bytes 18436

commit v5 on v4

--- a/solution.py
+++ b/solution.py
@@ -15,8 +15,8 @@
 EPS = 1e-05
 ALONG = (1, 7, 2, 6, 3, 5, 4)
 ACROSS = (4, 3, 5, 2, 6, 1, 7, 0)
-CROSS_ROWS = (0, 16, 0)
-ALONG_ROWS = (0, 14, 0)
+CROSS_ROWS = (4, 12, 0)
+ALONG_ROWS = (8, 6, 0)
 PASS_ROWS = (0, 14, 0)
 F32 = jnp.float32
 BF16 = jnp.bfloat16
@@ -562,21 +562,6 @@
             fin_recv[k] = fin_send[k]
 
 
-    for k in range(2):
-
-        @pl.when(jnp.logical_not(is_self(k)))
-        def _():
-            remote(fin_send.at[k], fin_recv.at[k], fin_s.at[k], fin_r.at[k], (f, r)).wait_recv()
-
-        out[32 * k : 32 * k + 32, :] = fin_recv[k]
-
-    for k in range(2):
-
-        @pl.when(jnp.logical_not(is_self(k)))
-        def _():
-            remote(hid.at[pl.ds(0, 32)], hid_all.at[r, k], h1_s.at[k], h1_r.at[k], (f, r)).wait_send()
-            remote(fin_send.at[k], fin_recv.at[k], fin_s.at[k], fin_r.at[k], (f, r)).wait_send()
-
     @pl.loop(1, R)
     def _(o):
         to = (r + o) % R
@@ -621,6 +606,21 @@
         @pl.when(first_user + m != r)
         def _():
             remote(gc_send, gc_recv.at[piece], gc_s.at[m], gc_r.at[piece], (f, r)).wait_send()
+
+    for k in range(2):
+
+        @pl.when(jnp.logical_not(is_self(k)))
+        def _():
+            remote(fin_send.at[k], fin_recv.at[k], fin_s.at[k], fin_r.at[k], (f, r)).wait_recv()
+
+        out[32 * k : 32 * k + 32, :] = fin_recv[k]
+
+    for k in range(2):
+
+        @pl.when(jnp.logical_not(is_self(k)))
+        def _():
+            remote(hid.at[pl.ds(0, 32)], hid_all.at[r, k], h1_s.at[k], h1_r.at[k], (f, r)).wait_send()
+            remote(fin_send.at[k], fin_recv.at[k], fin_s.at[k], fin_r.at[k], (f, r)).wait_send()
 
 
 def mixer(*operands):

time: 212 us -> 208 us (0.981)
  the two profiles are of different devices: /device:TPU:23 before, /device:TPU:21 now
where the time goes in v5:
time: 208 us
  Pallas kernels  201 us (97%)
  local copies, waits for them, and re-layouts  5.68 us (3%)
    pallas_call x1, Pallas kernels, mixer(): pl.pallas_call(kernel, out_shape=(jax.ShapeDtypeStruct((64, 128), BF16),...  201 us
    unnamed x8, local copies, waits for them, and re-layouts  5.68 us

profile of v5, /device:TPU:21, one launch (start us, length us, event | category | flops | bytes accessed | tf_op | source)
XLA Modules:
  0.0 208.0 jit_solution(10381917589417398376)
XLA Ops:
  1.3 201.0 %mixer.1 = (bf16[64,128]{1,0:T(8,128)(2,1)}, bf16[16,256,256]{2,1,0:T(8,128)(2,1)}, bf16[3,16,256]{2,1,0:T(8,128)(2,1)}, bf16[3,16,64]{2,1,0:T(8,128)(2,1)}) custom-call(s32[1]{0:T(128)S(6)} %copy.28.live_h, s32[16]{0:T(128)} %td_h.1, s32[16]{0:T(128)} %ts_h.1, f32[2]{0:T(128)} %sb_h.1, f32[2]{0:T(128)} %dr_h.1, f32[2]{0:T(128)} %sg_h.1, ...), custom_call_target="tpu_custom_call" | custom-call | tf_op jit(solution)/shard_map/mixer/pallas_call | solution.py:631
  202.3 1.3 copy.29
  203.7 0.0 copy-start
  203.7 0.0 copy-start.1
  203.7 3.1 %copy.30 = bf16[16,2,128,256]{3,2,1,0:T(8,128)(2,1)} copy(bf16[16,2,128,256]{3,2,1,0:T(8,128)(2,1)} %bitcast.14) | data formatting | bytes 4194304
  206.8 0.0 copy-done
  206.8 0.6 copy.31
  207.4 0.0 copy-done.1
  207.4 0.6 copy.32
Async XLA Ops:
  203.7 3.1 %copy-start = (bf16[3,16,256]{2,1,0:T(8,128)(2,1)S(1)}, bf16[3,16,256]{2,1,0:T(8,128)(2,1)}, u32[]{:S(2)}) copy-start(bf16[3,16,256]{2,1,0:T(8,128)(2,1)} %get-tuple-element.10) | copy-start | bytes 73732
  203.7 3.8 %copy-start.1 = (bf16[3,16,64]{2,1,0:T(8,128)(2,1)S(1)}, bf16[3,16,64]{2,1,0:T(8,128)(2,1)}, u32[]{:S(2)}) copy-start(bf16[3,16,64]{2,1,0:T(8,128)(2,1)} %get-tuple-element.11) | copy-start | bytes 18436
